TPU v7x, 32 devices: a whole 2x2x4 slice. The times are simulated.
32 devices in a mesh: dp: 16 (over z, x, core), mp: 2 (over y).
Axes of the slice: x: 2, y: 2, z: 4, core: 2. Of those that a mesh axis runs over, the one named last changes fastest.
Arguments:
- inputs: bfloat16 [16384, 768], P('dp'), may hold values from -6 to 6
- segment_ids: int32 [16384], P('dp'), may hold values from 0 to 6, as said below
- pad_flags: int32 [16384], P('dp'), may hold values from 0 to 1, as said below
- w_query: bfloat16 [768, 768], P(None, 'mp'), may hold values from -0.3125 to 0.3125
- w_key: bfloat16 [768, 768], P(None, 'mp'), may hold values from -0.3125 to 0.3125
- w_value: bfloat16 [768, 768], P(None, 'mp'), may hold values from -0.21875 to 0.21875
- b_query: float32 [768], P('mp'), may hold values from -3 to 3
- b_value: float32 [768], P('mp'), may hold values from -3 to 3
- w_proj: bfloat16 [768, 768], P('mp'), may hold values from -0.875 to 0.875
- b_proj: float32 [768], replicated, may hold values from -3 to 3
- gain_attn: float32 [768], replicated, may hold values from 0.5 to 1.5
- shift_attn: float32 [768], replicated, may hold values from -2 to 2
- w_up: bfloat16 [768, 3072], P(None, 'mp'), may hold values from -0.21875 to 0.21875
- b_up: float32 [3072], P('mp'), may hold values from -3 to 3
- w_down: bfloat16 [3072, 768], P('mp'), may hold values from -0.109375 to 0.109375
- b_down: float32 [768], replicated, may hold values from -3 to 3
- gain_ffn: float32 [768], replicated, may hold values from 0.5 to 1.5
- shift_ffn: float32 [768], replicated, may hold values from -2 to 2
- cotangent: bfloat16 [16384, 768], P('dp'), may hold values from -6 to 6
Outputs:
- outputs: bfloat16 [16384, 768], P('dp')
- grad_inputs: float32 [16384, 768], P('dp')
- grad_query: float32 [768, 768], P('dp', 'mp')
- grad_key: float32 [768, 768], P('dp', 'mp')
- grad_value: float32 [768, 768], P('dp', 'mp')
- grad_bquery: float32 [768], P('mp')
- grad_bvalue: float32 [768], P('mp')
- grad_proj: float32 [768, 768], P('mp', 'dp')
- grad_bproj: float32 [768], replicated
- grad_gain_attn: float32 [768], replicated
- grad_shift_attn: float32 [768], replicated
- grad_up: float32 [768, 3072], P('dp', 'mp')
- grad_bup: float32 [3072], P('mp')
- grad_down: float32 [3072, 768], P('mp', 'dp')
- grad_bdown: float32 [768], replicated
- grad_gain_ffn: float32 [768], replicated
- grad_shift_ffn: float32 [768], replicated
Inputs may be any that keep to these rules, and one draw needn't show every extreme that they name: `segment_ids`: within each aligned run of 512 tokens (one packed sequence) the ids start at 0 and never fall; the largest, 6, is reached in some sequence of every draw. `pad_flags`: 1 marks padding, which fills the last 1 to 128 tokens of every packed sequence.
All inputs are finite; a program needn't handle non-finite values.
Results may differ from a plain program's by a relative error of at most 0.013.
The roundings to bfloat16 on the way count: a program that leaves them out, or rounds other values in their place, can miss the bound.
Values sent between devices are 32-bit elements; how exact they have to be, the bound alone decides.
No kernel may reach another device: no remote copies, remote signals or barrier semaphores. Data moves between devices by JAX's collectives and lax.ppermute only.
A program may use at most 192 MiB of HBM per device.

v0:
```python
import functools
import math

import jax
import jax.numpy as jnp
from jax import lax
from jax.experimental import pallas as pl
from jax.experimental.pallas import tpu as pltpu
from jax.sharding import PartitionSpec as P

HD = 64
LENGTH = 512
QUERY_CHUNK = 256
UNIT_BLOCK = 512
BACK_BLOCK = 256
norm_eps = 1e-05
masked_value = -1000000000.0
BF = jnp.bfloat16
F32 = jnp.float32
VMEM_BYTES = 50 * 1024 * 1024


def nn(a, b):
    return lax.dot_general(a, b, (((1,), (0,)), ((), ())), preferred_element_type=F32)


def nt(a, b):
    return lax.dot_general(a, b, (((1,), (1,)), ((), ())), preferred_element_type=F32)


def call(body, grid, ins, outs, scratch=(), micros=1.0, alias=None):
    def spec(shape, block, index):
        if block == "smem":
            return pl.BlockSpec(memory_space=pltpu.SMEM)
        if block == "any":
            return pl.BlockSpec(memory_space=pl.ANY)
        if block is None:
            return pl.BlockSpec(shape, lambda *_: (0,) * len(shape))
        return pl.BlockSpec(block, index)

    moved = sum(a.size * a.dtype.itemsize for a, _, _ in ins)
    moved += sum(math.prod(s) * jnp.dtype(d).itemsize for s, d, _, _ in outs)
    return pl.pallas_call(
        body,
        grid=grid,
        in_specs=[spec(a.shape, b, i) for a, b, i in ins],
        out_specs=[spec(s, b, i) for s, _, b, i in outs],
        out_shape=[jax.ShapeDtypeStruct(s, d) for s, d, _, _ in outs],
        scratch_shapes=list(scratch),
        input_output_aliases=alias or {},
        compiler_params=pltpu.CompilerParams(vmem_limit_bytes=VMEM_BYTES),
        cost_estimate=pl.CostEstimate(
            flops=int(micros * 1.15e9), bytes_accessed=moved, transcendentals=0
        ),
    )(*[a for a, _, _ in ins])


def mask_bias(segc_ref, segr_ref, padc_ref, bias_ref):
    shape = bias_ref.shape
    key = lax.broadcasted_iota(jnp.int32, shape, 0)
    query = lax.broadcasted_iota(jnp.int32, shape, 1)
    same = segc_ref[...] == segr_ref[...]
    allowed = same & ((padc_ref[...] == 0) | (key == query))
    bias_ref[...] = jnp.where(allowed, 0.0, masked_value)


def attend_forward(
    x_ref, wq_ref, wk_ref, wv_ref, bq_ref, bv_ref, bu_ref, segc_ref, segr_ref, padc_ref,
    q_ref, k_ref, v_ref, ctx_ref, send_ref, lse_ref, bias_ref,
):
    x = x_ref[...]
    q_ref[...] = ((nn(x, wq_ref[...]) + bq_ref[...]).astype(BF).astype(F32) * HD ** (-0.5)).astype(BF)
    k_ref[...] = nn(x, wk_ref[...]).astype(BF)
    v_ref[...] = (nn(x, wv_ref[...]) + bv_ref[...]).astype(BF)
    mask_bias(segc_ref, segr_ref, padc_ref, bias_ref)
    length, wide = x.shape[0], q_ref.shape[1]
    if send_ref.shape[0] > length:
        send_ref[length:] = jnp.zeros((send_ref.shape[0] - length, wide), F32)
        for at in range(bu_ref.shape[1] // wide):
            send_ref[length + at:length + at + 1] = bu_ref[:, at * wide:(at + 1) * wide]

    def pair(index, carry):
        cols = pl.ds(pl.multiple_of(index * 128, 128), 128)
        keys = k_ref[:, cols]
        values_t = v_ref[:, cols].T
        lane = lax.broadcasted_iota(jnp.int32, (QUERY_CHUNK, 128), 1)
        for start in range(0, length, QUERY_CHUNK):
            rows = pl.ds(start, QUERY_CHUNK)
            query = q_ref[rows, cols]
            parts = []
            for head in range(2):
                one = jnp.where((lane < HD) == (head == 0), query, jnp.zeros_like(query))
                scores = nt(keys, one) + bias_ref[:, rows]
                highest = jnp.max(scores, axis=0, keepdims=True)
                grown = jnp.exp(scores - highest)
                total = jnp.sum(grown, axis=0, keepdims=True)
                weights = (grown * (1.0 / total)).astype(BF)
                lse_ref[pl.ds(2 * index + head, 1), rows] = highest + jnp.log(total)
                parts.append(nn(values_t[head * HD:(head + 1) * HD], weights))
            context = jnp.concatenate(parts, axis=0).T.astype(BF)
            ctx_ref[rows, cols] = context
            send_ref[rows, cols] = context.astype(F32)
        return carry

    lax.fori_loop(0, q_ref.shape[1] // 128, pair, 0)


def attend_backward(
    parts, q_ref, k_ref, v_ref, lse_ref, dctx_ref, segc_ref, segr_ref, padc_ref, wq_ref, wk_ref, wv_ref, *rest
):
    bias_ref, part_refs = rest[-1], rest[-1 - parts:-1]
    dqkv_ref, sums_ref = rest[-3 - parts:-1 - parts]
    mask_bias(segc_ref, segr_ref, padc_ref, bias_ref)
    length, width = q_ref.shape

    def pair(index, carry):
        first = pl.multiple_of(index * 128, 128)
        cols = pl.ds(first, 128)
        keys = k_ref[:, cols]
        values = v_ref[:, cols]
        keys_t = keys.T
        lane = lax.broadcasted_iota(jnp.int32, (QUERY_CHUNK, 128), 1)
        d_keys = [None, None]
        d_values = [None, None]
        for start in range(0, length, QUERY_CHUNK):
            rows = pl.ds(start, QUERY_CHUNK)
            query = q_ref[rows, cols]
            grad = dctx_ref[rows, cols]
            d_query = []
            for head in range(2):
                here = (lane < HD) == (head == 0)
                scores = nt(keys, jnp.where(here, query, jnp.zeros_like(query))) + bias_ref[:, rows]
                prob = jnp.exp(scores - lse_ref[pl.ds(2 * index + head, 1), rows])
                weights = prob.astype(BF)
                d_prob = nt(values, jnp.where(here, grad, jnp.zeros_like(grad)))
                inner = jnp.sum(prob * d_prob, axis=0, keepdims=True)
                raw = (prob * (d_prob - inner)).astype(BF)
                dv = nn(weights, grad)
                dk = nn(raw, query)
                d_values[head] = dv if start == 0 else d_values[head] + dv
                d_keys[head] = dk if start == 0 else d_keys[head] + dk
                d_query.append(nn(keys_t[head * HD:(head + 1) * HD], raw))
            dq = (jnp.concatenate(d_query, axis=0).T * HD ** (-0.5)).astype(BF)
            dqkv_ref[rows, cols] = dq
        full = lax.broadcasted_iota(jnp.int32, (length, 128), 1) < HD
        dqkv_ref[:, pl.ds(pl.multiple_of(width + first, 128), 128)] = jnp.where(
            full, d_keys[0], d_keys[1]
        ).astype(BF)
        dqkv_ref[:, pl.ds(pl.multiple_of(2 * width + first, 128), 128)] = jnp.where(
            full, d_values[0], d_values[1]
        ).astype(BF)
        return carry

    lax.fori_loop(0, width // 128, pair, 0)
    sums_ref[...] = jnp.broadcast_to(
        jnp.sum(dqkv_ref[...].astype(F32), axis=0, keepdims=True), sums_ref.shape
    )
    total = None
    for part, weight in enumerate((wq_ref, wk_ref, wv_ref)):
        term = nt(dqkv_ref[:, part * width:(part + 1) * width], weight[...])
        total = term if total is None else total + term
    at = 0
    for part_ref in part_refs:
        part_ref[...] = total[at:at + part_ref.shape[0]]
        at += part_ref.shape[0]


def moments(values):
    average = jnp.mean(values, axis=-1, keepdims=True)
    centered = values - average
    variance = jnp.mean(centered * centered, axis=-1, keepdims=True)
    inverse = lax.rsqrt(variance + norm_eps)
    return centered * inverse, inverse


def norm_backward(upstream, n, inverse, gain):
    scaled = upstream * gain
    return inverse * (
        scaled
        - jnp.mean(scaled, axis=-1, keepdims=True)
        - n * jnp.mean(scaled * n, axis=-1, keepdims=True)
    )


def down_sum(values):
    return jnp.sum(values, axis=0, keepdims=True)


def activate(nlow, wu_ref, bias, act_ref, slope_ref):
    up = nn(nlow, wu_ref[...]) + bias
    cdf = 0.5 * (1.0 + lax.erf(up * 2.0 ** (-0.5)))
    active = (up * cdf).astype(BF)
    act_ref[...] = active
    slope = cdf + up * jnp.exp(-0.5 * up * up) * (1.0 / math.sqrt(2.0 * math.pi))
    slope_ref[...] = slope.astype(BF)
    return active


def feed_own(
    x_ref, co_ref, cx_ref, wpo_ref, wpx_ref, bp_ref, g_ref, s_ref, bd_ref, wu_ref, bu_ref, wd_ref, *rest
):
    nlow_ref, acc_ref, hid_ref, act_ref, slope_ref = rest[-5:]

    @pl.when(pl.program_id(0) == 0)
    def _():
        attn = nn(co_ref[...], wpo_ref[...]) + nt(cx_ref[:x_ref.shape[0]].astype(BF), wpx_ref[...]) + bp_ref[...]
        hidden = x_ref[...].astype(F32) + attn
        hid_ref[...] = hidden
        n, _ = moments(hidden)
        normed = n * g_ref[...] + s_ref[...]
        nlow_ref[...] = normed.astype(BF)
        acc_ref[...] = normed + bd_ref[...]

    acc_ref[...] += nn(activate(nlow_ref[...], wu_ref, bu_ref[...], act_ref, slope_ref), wd_ref[...])


def feed_up(nlow_ref, wu_ref, bu_ref, *rest):
    bias = bu_ref[pl.ds(pl.program_id(0), 1), :]
    activate(nlow_ref[...], wu_ref, bias, *rest[-2:])


def feed_down(
    act_ref, starta_ref, startb_ref, wd_ref, g_ref, s_ref, cot_ref,
    out_ref, dsum_ref, dffn_ref, stats_ref, low_ref,
):
    weights = wd_ref[...].astype(BF)
    low_ref[...] = weights
    stats_ref[...] = jnp.zeros_like(stats_ref)
    length = starta_ref.shape[0]
    for at, start_ref in enumerate((starta_ref, startb_ref)):
        rows = pl.ds(at * length, length)
        total = start_ref[...] + nt(act_ref[rows, :], weights)
        n, inverse = moments(total)
        out_ref[rows, :] = (n * g_ref[...] + s_ref[...]).astype(BF)
        cot = cot_ref[rows, :].astype(F32)
        d_summed = norm_backward(cot, n, inverse, g_ref[...])
        d_ffn = d_summed.astype(BF)
        dsum_ref[rows, :] = d_summed
        dffn_ref[rows, :] = d_ffn
        stats_ref[0:1] += down_sum(cot * n)
        stats_ref[1:2] += down_sum(cot)
        stats_ref[2:3] += down_sum(d_ffn.astype(F32))


def feed_backward(
    dffn_ref, so_ref, sx_ref, wdo_ref, wdx_ref, wuo_ref, wux_ref, dsum_ref, hid_ref, g_ref, wpo_ref,
    duo_ref, bup_ref, dhid_ref, dattn_ref, dctx_ref, stats_ref, acc_ref,
):
    @pl.when(pl.program_id(0) == 0)
    def _():
        acc_ref[...] = dsum_ref[...]

    d_ffn = dffn_ref[...]
    d_own = (nt(d_ffn, wdo_ref[...]) * so_ref[...].astype(F32)).astype(BF)
    d_other = (nn(d_ffn, wdx_ref[...]) * sx_ref[...].astype(F32)).astype(BF)
    duo_ref[...] = d_own
    bup_ref[...] = jnp.broadcast_to(down_sum(d_own.astype(F32)), bup_ref.shape)
    acc_ref[...] += nt(d_own, wuo_ref[...]) + nt(d_other, wux_ref[...])

    @pl.when(pl.program_id(0) == pl.num_programs(0) - 1)
    def _():
        d_normed = acc_ref[...]
        n, inverse = moments(hid_ref[...])
        d_hidden = norm_backward(d_normed, n, inverse, g_ref[...])
        d_attn = d_hidden.astype(BF)
        dhid_ref[...] = d_hidden
        dattn_ref[...] = d_attn
        dctx_ref[...] = nt(d_attn, wpo_ref[...]).astype(BF)
        stats_ref[...] = jnp.zeros_like(stats_ref)
        stats_ref[0:1] = down_sum(d_normed * n)
        stats_ref[1:2] = down_sum(d_normed)
        stats_ref[2:3] = down_sum(d_attn.astype(F32))


def input_total(parts, dhid_ref, *refs):
    at = 0
    for mine_ref, theirs_ref in zip(refs[:parts], refs[parts:2 * parts]):
        rows = pl.ds(at, mine_ref.shape[0])
        refs[-1][rows, :] = dhid_ref[rows, :] + (mine_ref[...] + theirs_ref[...])
        at += mine_ref.shape[0]


def scatter_rows(g, first, keep_ref, send_ref, rows, extra=None):
    over, across = keep_ref.shape[1:3]
    for block in range(keep_ref.shape[0] * over * across):
        at = 2 * block * rows
        even, odd = g[at:at + rows], g[at + rows:at + 2 * rows]
        place = (block // (over * across), block // across % over, block % across)
        keep_ref[place + (slice(0, rows),)] = jnp.where(first, even, odd)
        send_ref[place + (slice(0, rows),)] = jnp.where(first, odd, even)
        if extra is not None:
            keep_ref[place + (slice(rows, None),)] = extra
            send_ref[place + (slice(rows, None),)] = extra


def put(g, core_ref, outs, rows, extra=None):
    if len(outs) == 2:
        scatter_rows(g, core_ref[0] == 0, *outs, rows, extra)
    else:
        outs[0][:g.shape[0]] = g
        if extra is not None:
            outs[0][g.shape[0]:] = extra


def turn(refs, turned, step=0):
    @pl.when(pl.program_id(0) == step)
    def _():
        at = 0
        for ref in refs:
            turned[:, at:at + ref.shape[0]] = ref[...].T
            at += ref.shape[0]


def gradient(left_ref, right_ref, out_ref, turned):
    turn((left_ref,), turned)
    out_ref[...] = nn(turned[...], right_ref[...])


def gradient_up(rows, core_ref, la_ref, lb_ref, right_ref, proj_ref, ca_ref, cb_ref, *rest):
    turned, outs = rest[-1], rest[:-1]
    last = pl.num_programs(0) - 1
    count = len(outs) // 2
    length = la_ref.shape[0]
    turn((la_ref, lb_ref), turned)
    turn((proj_ref,), turned, last)

    @pl.when(pl.program_id(0) < last // 2)
    def _():
        put(nn(turned[...], right_ref[...]), core_ref, outs[:count], rows)

    @pl.when((pl.program_id(0) >= last // 2) & (pl.program_id(0) < last))
    def _():
        put(nn(turned[...], right_ref[...]), core_ref, outs[count:], rows)

    @pl.when(pl.program_id(0) == last)
    def _():
        g = nn(turned[:, :length], ca_ref[...]) + nn(turned[:, length:], cb_ref[...])
        put(g, core_ref, outs[count:], rows)


def gradient_attention(
    rows, core_ref, x_ref, dqkv_ref, f_ref, a_ref, up_ref, ka_ref, kb_ref, *rest
):
    turned, outs = rest[-1], rest[:-1]
    count = len(outs) // 2
    width = x_ref.shape[1]
    half = width // 2
    up, qkv = up_ref[...], ka_ref[...] + kb_ref[...]
    pieces = [f_ref[:3], a_ref[:3]] + [
        up[:1, at * width:(at + 1) * width] for at in range(up.shape[1] // width)
    ] + [jnp.concatenate([qkv[:1, :half], qkv[:1, 2 * half:]], axis=1)]
    have = sum(piece.shape[0] for piece in pieces)
    pieces.append(jnp.zeros((-have % 16, width), F32))
    extra = jnp.concatenate(pieces, axis=0)
    turn((x_ref,), turned)
    put(nn(turned[...], dqkv_ref[:, :2 * half]), core_ref, outs[:count], rows, extra)
    put(nn(turned[...], dqkv_ref[:, 2 * half:]), core_ref, outs[count:], rows)


def join_pieces(place_ref, *refs):
    out_ref = refs[-1]
    rows = refs[0].shape[0]
    for mine in (True, False):
        base = (place_ref[0] if mine else 1 - place_ref[0]) * 4
        pieces = refs[:5] if mine else refs[5:10]
        starts = [base + jnp.bitwise_xor(place_ref[1], piece) for piece in (0, 1, 2, 3, 3)]
        for index, (at, piece) in enumerate(zip(starts, pieces)):
            start = at * rows + (rows // 2 if index == 4 else 0)
            out_ref[pl.ds(pl.multiple_of(start, 16), piece.shape[0])] = piece[...].astype(BF)


def pick(array, index, axis):
    return lax.dynamic_index_in_dim(array, index, axis, keepdims=False)


def lock(*values):
    return lax.optimization_barrier(values)


def on_device(
    dp, inputs, segment_ids, pad_flags, w_query, w_key, w_value, b_query, b_value, w_proj, b_proj,
    gain_attn, shift_attn, w_up, b_up, w_down, b_down, gain_ffn, shift_ffn, cotangent,
):
    d = lax.axis_index("dp")
    tokens, width = inputs.shape
    half = w_query.shape[1]
    units = w_up.shape[1]
    core, low = d % 2, (d // 2) % 4
    pair = range(tokens // LENGTH)

    def swap_mp(array):
        return lax.ppermute(array, "mp", [(0, 1), (1, 0)])

    def swap_dp(array, bit):
        return lax.ppermute(array, "dp", [(i, i ^ bit) for i in range(dp)])

    def row(vector):
        return vector.reshape(1, -1)

    full = lambda array: (array, None, None)

    rows = width // 8
    place_d = jnp.stack([core, low]).astype(jnp.int32)

    def eighth(weight):
        return lax.dynamic_slice_in_dim(weight, (core * 4 + low) * rows, rows, 0).astype(F32)

    def eighth_t(weight):
        return lax.dynamic_slice_in_dim(weight, (core * 4 + low) * rows, rows, 1).T.astype(F32)

    def near_pieces(own):
        return swap_dp(own, 2), swap_dp(own, 4)

    def far_pieces(by_x, by_z):
        return swap_dp(by_z[:rows // 2], 2), swap_dp(by_x[rows // 2:], 4)

    def join(mine, theirs):
        (joined,) = call(
            join_pieces, (1,), [(place_d, "smem", None)] + [full(a) for a in mine + theirs],
            [((width, mine[0].shape[1]), BF, None, None)],
            micros=3.0,
        )
        return joined

    def other_core(pieces):
        return tuple(swap_dp(piece, 1) for piece in pieces)

    def tokens_of(array, at):
        return lax.slice_in_dim(array, at * LENGTH, (at + 1) * LENGTH, axis=0)

    def sequence(array, at):
        return (array, (LENGTH, array.shape[1]), lambda *_: (at, 0))

    square = pltpu.VMEM((LENGTH, LENGTH), F32)
    heads = half // HD
    lanes = (LENGTH, half)
    masks = []
    for at in pair:
        seg, pad = tokens_of(segment_ids, at), tokens_of(pad_flags, at)
        masks.append([full(seg.reshape(-1, 1)), full(row(seg)), full(pad.reshape(-1, 1))])
    own_qkv = [full(w_query), full(w_key), full(w_value)]

    def attend(at, token):
        return call(
            attend_forward, (1,),
            [sequence(token, at)] + own_qkv + [full(row(b_query)), full(row(b_value)), full(row(b_up))]
            + masks[at],
            [(lanes, BF, None, None)] * 4
            + [((LENGTH + 8 * (at == 0), half), F32, None, None), ((heads, LENGTH), F32, None, None)],
            [square], micros=9.0,
        )

    shard = width // dp
    (proj,) = lock(swap_mp(eighth_t(w_proj)))
    down_y = swap_mp(lax.dynamic_slice_in_dim(w_down, d * shard, shard, 1).T.astype(F32))
    saved = [attend(0, lock(inputs, proj)[0])]
    proj, proj_near, up, down_y, saved[0] = lock(
        proj, near_pieces(proj), swap_mp(lock(eighth(w_up), proj)[0]), down_y, tuple(saved[0])
    )
    down_oth = lax.all_gather(down_y, "dp", axis=0, tiled=True)
    saved.append(attend(1, lock(inputs, proj)[0]))
    proj = (proj,) + tuple(proj_near)
    proj_far = far_pieces(*proj_near)
    ctx_a, up_near, proj_far, proj_core, saved[1] = lock(
        swap_mp(saved[0][4]), near_pieces(up), proj_far, other_core(proj), tuple(saved[1])
    )
    proj_far, proj_far_core, proj, proj_core = lock(
        proj_far, other_core(proj_far), proj, proj_core
    )

    steps = units // UNIT_BLOCK
    unit_row = lambda array: (array, (1, UNIT_BLOCK), lambda i: (0, i))
    unit_col = lambda array: (array, (array.shape[0], UNIT_BLOCK), lambda i: (0, i))
    unit_block = lambda array: (array, (UNIT_BLOCK, width), lambda i: (i, 0))
    unit_all = lambda array, block: (array, (array.shape[0], block), lambda i: (0, i))
    column = lambda array: (array, (array.shape[0], half), lambda i: (0, i))
    token = lambda dtype: ((LENGTH, width), dtype, None, None)
    stat = ((8, width), F32, None, None)
    def rows_of(at, cols, dtype, block=None):
        if block is None:
            return ((tokens, cols), dtype, (LENGTH, cols), lambda *_: (at, 0))
        return ((tokens, cols), dtype, (LENGTH, block), lambda i: (at, i))

    proj_oth = join(proj + tuple(proj_far), proj_core + tuple(proj_far_core))

    def forward_own(at, context, before):
        outs = call(
            feed_own, (steps,),
            [sequence(inputs, at), full(saved[at][3]), full(context), full(w_proj), full(proj_oth),
             full(row(b_proj)), full(row(gain_attn)), full(row(shift_attn)), full(row(b_down)),
             unit_col(w_up), unit_row(row(b_up)), unit_block(w_down)]
            + [(array, "any", None) for array in before],
            [token(BF), token(F32), rows_of(at, width, F32), rows_of(at, units, BF, UNIT_BLOCK),
             rows_of(at, units, BF, UNIT_BLOCK)],
            micros=8.0, alias={12 + i: 2 + i for i in range(len(before))},
        )
        return outs[0], outs[1], outs[2:]

    def forward_other(at, normed, before):
        return call(
            feed_up, (units // half,),
            [full(normed), column(joined), (ctx_a, (8, half), lambda i: (LENGTH // 8, 0))]
            + [(array, "any", None) for array in before],
            [rows_of(at, units, BF, half)] * 2, micros=4.0,
            alias={3 + i: i for i in range(len(before))},
        )

    normed_a, partial_a, kept = forward_own(0, ctx_a, ())
    up = (up,) + tuple(up_near)
    ctx_b, up_far, up_core, normed_a, partial_a, kept = lock(
        swap_mp(saved[1][4]), far_pieces(*up_near), other_core(up), normed_a, partial_a, tuple(kept)
    )
    up, up_far, up_far_core, up_core, normed_a, ctx_b = lock(
        up, up_far, other_core(up_far), up_core, normed_a, ctx_b
    )
    joined = join(up + tuple(up_far), up_core + tuple(up_far_core))
    other = forward_other(0, normed_a, ())
    normed_b, partial_b, (hidden, act_own, slope_own) = forward_own(1, ctx_b, kept)
    act_oth, slope_oth = forward_other(1, normed_b, other)
    every = lambda dtype: ((tokens, width), dtype, None, None)
    outputs, d_summed, d_ffn, stats_ffn, down_oth = call(
        feed_down, (1,),
        [full(act_oth), full(partial_a), full(partial_b), full(down_oth), full(row(gain_ffn)),
         full(row(shift_ffn)), full(cotangent)],
        [every(BF), every(F32), every(BF), stat, ((width, units), BF, None, None)], micros=10.0,
    )

    split = dp == 16
    core_arg = jnp.reshape(core, (1,)).astype(jnp.int32)
    lead = (2, dp // 8, 2, width // dp)
    turned = pltpu.VMEM((width, tokens), BF)

    def parted(cols, block, index, extra=0):
        if not split:
            out = ((width + extra, cols), F32, (width + extra, block), lambda i: (0, index(i)))
            return [out]
        shape = lead[:-1] + (lead[-1] + extra,)
        return [(shape + (cols,), F32, shape + (block,), lambda i: (0, 0, 0, 0, index(i)))] * 2

    def pairs(outs):
        return outs[:len(outs) // 2], outs[len(outs) // 2:]

    bits = {"x": (d // 2) % 2, "l": (d // 4) % 2, "u": d // 8}
    hops = {"x": 2, "l": 4, "u": 8}

    class Reduction:
        def __init__(self, parts, order, terms=None):
            self.names = ["u", "l", "x"]
            self.order, self.parts, self.terms = list(order), parts, terms

        def step(self):
            if not split:
                return self.parts[0]
            if self.terms is None:
                got = swap_dp(self.parts[1], 1)
                self.terms = [self.parts[0], got]
                return got
            stage = self.order.pop(0)
            axis = self.names.index(stage)
            self.names.pop(axis)
            bit = bits[stage]
            send = sum(pick(term, 1 - bit, axis) for term in self.terms)
            got = swap_dp(send, hops[stage])
            self.terms = [pick(term, bit, axis) for term in self.terms] + [got]
            return got

        def result(self):
            if not split:
                return lax.psum_scatter(self.parts[0], "dp", scatter_dimension=0, tiled=True)
            while self.order:
                self.step()
            return sum(self.terms)

    (down_whole,) = call(
        gradient, (units // UNIT_BLOCK,), [full(d_ffn), unit_all(act_own, UNIT_BLOCK)],
        [((width, units), F32, (width, UNIT_BLOCK), lambda i: (0, i))], [turned], 6.0,
    )
    d_ffn, down_whole = lock(d_ffn, down_whole)
    down_part = lax.psum_scatter(down_whole, "dp", scatter_dimension=0, tiled=True)
    back = lambda array: (array, (array.shape[0], BACK_BLOCK), lambda i: (0, i))
    d_up, sums_up, d_hidden, d_attn, d_context, stats_attn = call(
        feed_backward, (units // BACK_BLOCK,),
        [full(d_ffn), back(slope_own), back(slope_oth),
         (w_down, (BACK_BLOCK, width), lambda i: (i, 0)), back(down_oth), back(w_up), back(joined),
         full(d_summed), full(hidden), full(row(gain_attn)), full(w_proj)],
        [((tokens, units), BF, (tokens, BACK_BLOCK), lambda i: (0, i)),
         ((8, units), F32, (8, BACK_BLOCK), lambda i: (0, i)), every(F32), every(BF),
         ((tokens, half), BF, None, None), stat],
        [pltpu.VMEM((tokens, width), F32)], micros=20.0,
    )

    def back_attend(at, grad, before, sizes):
        q, k, v, _, _, lse = saved[at]
        outs = call(
            functools.partial(attend_backward, len(sizes)), (1,),
            [full(q), full(k), full(v), full(lse), sequence(grad, at)] + masks[at] + own_qkv
            + [(array, "any", None) for array in before],
            [rows_of(at, 3 * half, BF), ((8, 3 * half), F32, None, None)]
            + [((size, width), F32, None, None) for size in sizes],
            [square], micros=9.0, alias={11: 0} if before else {},
        )
        return outs[0], outs[1], list(outs[2:])

    blocks = units // half
    up = call(
        functools.partial(gradient_up, lead[-1]), (blocks + 1,),
        [(core_arg, "smem", None), full(normed_a), full(normed_b),
         (d_up, (tokens, half), lambda i: (0, jnp.minimum(i, blocks - 1))), full(d_attn),
         full(saved[0][3]), full(saved[1][3])],
        parted(units // 2, half, lambda i: jnp.minimum(i, blocks // 2 - 1))
        + parted(units // 2 + half, half, lambda i: jnp.maximum(i - blocks // 2, 0)),
        [turned], 9.0,
    )
    up, d_context = lock(up, d_context)
    up = [Reduction(parts, order) for parts, order in zip(pairs(up), ("lux", "xlu"))]

    def advance(reductions, *values):
        for one in reductions:
            one.step()
        if not split:
            return lock(*values)
        terms, *values = lock([one.terms for one in reductions], *values)
        for one, changed in zip(reductions, terms):
            one.terms = list(changed)
        return values

    dqkv, sums_a, mine_a = back_attend(0, d_context, (), (256, 256))
    dqkv, mine_a, d_context = advance(up, dqkv, mine_a, d_context)
    theirs_a = [swap_mp(mine_a[0])]
    dqkv, sums_b, mine_b = back_attend(1, d_context, (dqkv,), (128, 256, 128))
    dqkv, mine_a, mine_b, theirs_a = advance(up, dqkv, mine_a, mine_b, theirs_a)
    theirs_a.append(swap_mp(mine_a[1]))
    last = call(
        functools.partial(gradient_attention, lead[-1]), (1,),
        [(core_arg, "smem", None), full(inputs), full(dqkv)]
        + [full(a) for a in (stats_ffn, stats_attn, sums_up, sums_a, sums_b)],
        parted(2 * half, 2 * half, lambda i: 0, 16) + parted(half, half, lambda i: 0),
        [turned], 7.0,
    )
    last, mine_b, theirs_a = advance(up, last, mine_b, theirs_a)
    query, value = [Reduction(parts, order) for parts, order in zip(pairs(last), ("xlu", "lux"))]
    theirs_b = []
    for moving in (up + [query, value], [query, value], [query, value]):
        theirs_b.append(swap_mp(mine_b[len(theirs_b)]))
        mine_b, theirs_b = advance(moving, mine_b, theirs_b)
    if split:
        query_part, value_part = query.result(), value.result()
        vectors = query_part[shard:]
    else:
        (whole,) = query.parts
        vectors = lax.psum(whole[width:], "dp")
        query_part = lax.psum_scatter(whole[:width], "dp", scatter_dimension=0, tiled=True)
        value_part = value.result()
    query_part = query_part[:shard]
    up_part = [one.result() for one in up]
    proj_part = up_part[1][:, units // 2:]
    up_part = jnp.concatenate([up_part[0], up_part[1][:, :units // 2]], axis=1)

    grad_inputs = None
    for at, (mine, theirs) in enumerate(((mine_a, theirs_a), (mine_b, theirs_b))):
        ins = [sequence(d_hidden, at)] + [full(a) for a in list(mine) + list(theirs)]
        before = len(ins)
        if grad_inputs is not None:
            ins.append((grad_inputs, "any", None))
        (grad_inputs,) = call(
            functools.partial(input_total, len(mine)), (1,), ins, [rows_of(at, width, F32)],
            micros=2.5, alias={} if at == 0 else {before: 0},
        )
    return (
        outputs,
        grad_inputs,
        query_part[:, :half],
        query_part[:, half:],
        value_part,
        vectors[8, :half],
        vectors[8, half:],
        proj_part.T,
        vectors[5],
        vectors[3],
        vectors[4],
        up_part,
        vectors[6:8].reshape(-1),
        down_part.T,
        vectors[2],
        vectors[0],
        vectors[1],
    )


def solution(mesh):
    placed = (
        P("dp", None), P("dp"), P("dp"), P(None, "mp"), P(None, "mp"), P(None, "mp"), P("mp"),
        P("mp"), P("mp", None), P(), P(), P(), P(None, "mp"), P("mp"), P("mp", None), P(), P(), P(),
        P("dp", None),
    )
    return jax.shard_map(
        functools.partial(on_device, mesh.shape["dp"]),
        mesh=mesh,
        in_specs=placed,
        out_specs=(
            P("dp", None), P("dp", None), P("dp", "mp"), P("dp", "mp"), P("dp", "mp"), P("mp"),
            P("mp"), P("mp", "dp"), P(), P(), P(), P("dp", "mp"), P("mp"), P("mp", "dp"), P(), P(),
            P(),
        ),
        check_vma=False,
    )
```

profile of v0, /device:TPU:0, one launch (start us, length us, event | category | flops | bytes accessed | tf_op | source)
XLA Modules:
  0.0 319.5 jit_solution(13296466816907319786)
XLA Ops:
  21.2 10.0 %shard_map.314 = (bf16[512,384]{1,0:T(8,128)(2,1)S(1)}, bf16[512,384]{1,0:T(8,128)(2,1)S(1)}, bf16[512,384]{1,0:T(8,128)(2,1)S(1)}, bf16[512,384]{1,0:T(8,128)(2...) custom-call(bf16[1024,768]{1,0:T(8,128)(2,1)} %x_ref.7, bf16[768,384]{1,0:T(8,128)(2,1)S(1)} %copy-done.4, ...), custom_call_target="tpu_custom_call" | custom-call | flops 10350000128 | bytes 5741568 | tf_op jit(solution)/shard_map/pallas_call | solution.py:43
  44.7 9.9 %shard_map.315 = (bf16[512,384]{1,0:T(8,128)(2,1)S(1)}, bf16[512,384]{1,0:T(8,128)(2,1)S(1)}, bf16[512,384]{1,0:T(8,128)(2,1)S(1)}, bf16[512,384]{1,0:T(8,128)(2...) custom-call(bf16[1024,768]{1,0:T(8,128)(2,1)} %x_ref.7, bf16[768,384]{1,0:T(8,128)(2,1)S(1)} %copy-done.4, ...), custom_call_target="tpu_custom_call" | custom-call | flops 10350000128 | bytes 5729280 | tf_op jit(solution)/shard_map/pallas_call | solution.py:43
  58.6 6.8 %collective-permute-done.7.refs_2_ = f32[96,1536]{1,0:T(8,128)S(1)} collective-permute-done((f32[96,1536]{1,0:T(8,128)}, f32[96,1536]{1,0:T(8,128)S(1)}, u32[]{:S(2)}, u32[]{:S(2)}) %collective-permute-start.7) | collective-permute-done | bytes 589856 | tf_op jit(solution)/shard_map/ppermute | solution.py:395
  72.0 8.8 %shard_map.317 = (bf16[512,768]{1,0:T(8,128)(2,1)S(1)}, f32[512,768]{1,0:T(8,128)}, f32[1024,768]{1,0:T(8,128)}, bf16[1024,1536]{1,0:T(8,128)(2,1)}, bf16[1024,1536]{1,0:T(8,128)(2,1)}) custom-call(bf16[1024,768]{1,0:T(8,128)(2,1)} %x_ref.7, bf16[512,384]{1,0:T(8,128)(2,1)S(1)} %copy-done.22, f32[520,384]{1,0:T(8,128)S(1)} %collective-permute-done.5.cx_ref.bu_ref, ...), custom_call_target="tpu_custom_call" | custom-call | flops 9200000000 | bytes 20477952 | tf_op jit(solution)/shard_map/pallas_call | solution.py:43
  82.1 8.5 %collective-permute-done.15.refs_4_ = f32[48,1536]{1,0:T(8,128)S(1)} collective-permute-done((f32[48,1536]{1,0:T(8,128)S(1)}, f32[48,1536]{1,0:T(8,128)S(1)}, u32[]{:S(2)}, u32[]{:S(2)}) %collective-permute-start.15) | collective-permute-done | bytes 294944 | tf_op jit(solution)/shard_map/ppermute | solution.py:395
  97.5 4.6 %shard_map.320 = (bf16[1024,1536]{1,0:T(8,128)(2,1)}, bf16[1024,1536]{1,0:T(8,128)(2,1)}) custom-call(bf16[512,768]{1,0:T(8,128)(2,1)S(1)} %get-tuple-element.288.nlow_ref.la_ref, bf16[768,1536]{1,0:T(8,128)(2,1)S(1)} %copy-done.8, f32[520,384]{1,0:T(8,128)S(1)} %collective-permute-done.5.cx_ref.bu_ref), custom_call_target="tpu_custom_call" | custom-call | flops 4600000000 | bytes 10235904 | tf_op jit(solution)/shard_map/pallas_call | solution.py:43
  102.0 8.7 %shard_map.318 = (bf16[512,768]{1,0:T(8,128)(2,1)S(1)}, f32[512,768]{1,0:T(8,128)}, f32[1024,768]{1,0:T(8,128)}, bf16[1024,1536]{1,0:T(8,128)(2,1)}, bf16[1024,1536]{1,0:T(8,128)(2,1)}) custom-call(bf16[1024,768]{1,0:T(8,128)(2,1)} %x_ref.7, bf16[512,384]{1,0:T(8,128)(2,1)S(1)} %copy-done.18, ...), custom_call_target="tpu_custom_call", output_to_operand_aliasing={{2}: (12, {}), {3}: (13, {}), {4}: (14, {})} | custom-call | flops 9200000000 | bytes 29902848 | tf_op jit(solution)/shard_map/pallas_call | solution.py:43
  110.7 4.8 %shard_map.321 = (bf16[1024,1536]{1,0:T(8,128)(2,1)}, bf16[1024,1536]{1,0:T(8,128)(2,1)}) custom-call(bf16[512,768]{1,0:T(8,128)(2,1)S(1)} %get-tuple-element.277.nlow_ref.lb_ref, bf16[768,1536]{1,0:T(8,128)(2,1)S(1)} %copy-done.9, f32[520,384]{1,0:T(8,128)S(1)} %collective-permute-done.5.cx_ref.bu_ref, ...), custom_call_target="tpu_custom_call", output_to_operand_aliasing={{0}: (3, {}), {1}: (4, {})} | custom-call | flops 4600000000 | bytes 16527360 | tf_op jit(solution)/shard_map/pallas_call | solution.py:43
  117.8 11.5 %shard_map.322 = (bf16[1024,768]{1,0:T(8,128)(2,1)}, f32[1024,768]{1,0:T(8,128)}, bf16[1024,768]{1,0:T(8,128)(2,1)S(1)}, f32[8,768]{1,0:T(8,128)S(1)}, bf16[768,1536]{1,0:T(8,128)(2,1)}) custom-call(bf16[1024,1536]{1,0:T(8,128)(2,1)} %get-tuple-element.291.act_ref, f32[512,768]{1,0:T(8,128)S(1)} %copy-done.15, f32[512,768]{1,0:T(8,128)} %get-tuple-element.293.startb_ref, ...), custom_call_target="tpu_custom_call" | custom-call | flops 11500000256 | bytes 21264384 | tf_op jit(solution)/shard_map/pallas_call | solution.py:43
  129.3 6.8 %shard_map.323 = f32[768,1536]{1,0:T(8,128)} custom-call(bf16[1024,768]{1,0:T(8,128)(2,1)S(1)} %get-tuple-element.298.left_ref.dffn_ref, bf16[1024,1536]{1,0:T(8,128)(2,1)} %get-tuple-element.297.right_ref), custom_call_target="tpu_custom_call" | custom-call | flops 6899999744 | bytes 9437184 | tf_op jit(solution)/shard_map/pallas_call | solution.py:43
  137.3 20.4 %shard_map.324 = (bf16[1024,1536]{1,0:T(8,128)(2,1)}, f32[8,1536]{1,0:T(8,128)S(1)}, f32[1024,768]{1,0:T(8,128)}, bf16[1024,768]{1,0:T(8,128)(2,1)S(1)}, bf16[10...) custom-call(bf16[1024,768]{1,0:T(8,128)(2,1)} %copy-done.12, bf16[1024,1536]{1,0:T(8,128)(2,1)} %get-tuple-element.299.so_ref, ...), custom_call_target="tpu_custom_call" | custom-call | flops 23000000512 | bytes 32910336 | tf_op jit(solution)/shard_map/pallas_call | solution.py:43
  159.7 9.7 %shard_map.325 = (f32[2,2,2,48,768]{4,3,2,1,0:T(8,128)S(1)}, f32[2,2,2,48,768]{4,3,2,1,0:T(8,128)}, f32[2,2,2,48,1152]{4,3,2,1,0:T(8,128)}, f32[2,2,2,48,1152]{4,3,2,1,0:T(8,128)}) custom-call(s32[1]{0:T(128)} %bitcast.8.core_ref, bf16[512,768]{1,0:T(8,128)(2,1)S(1)} %copy-done.14, bf16[512,768]{1,0:T(8,128)(2,1)S(1)} %copy-done.11, ...), custom_call_target="tpu_custom_call" | custom-call | flops 10350000128 | bytes 12976132 | tf_op jit(solution)/shard_map/pallas_call | solution.py:43
  176.4 10.7 %shard_map.326 = (bf16[1024,1152]{1,0:T(8,128)(2,1)}, f32[8,1152]{1,0:T(8,128)S(1)}, f32[256,768]{1,0:T(8,128)}, f32[256,768]{1,0:T(8,128)}) custom-call(bf16[512,384]{1,0:T(8,128)(2,1)S(1)} %copy-done.31, bf16[512,384]{1,0:T(8,128)(2,1)S(1)} %copy-done.33, bf16[512,384]{1,0:T(8,128)(2,1)S(1)} %copy-done.35, f32[6,512]{1,0:T(8,128)S(1)} %get-tuple-element.319.lse_ref, ...), custom_call_target="tpu_custom_call" | custom-call | flops 10350000128 | bytes 7723008 | tf_op jit(solution)/shard_map/pallas_call | solution.py:43
  192.6 10.7 %shard_map.327 = (bf16[1024,1152]{1,0:T(8,128)(2,1)}, f32[8,1152]{1,0:T(8,128)S(1)}, f32[128,768]{1,0:T(8,128)S(1)}, f32[256,768]{1,0:T(8,128)}, f32[128,768]{1,0:T(8,128)S(1)}) custom-call(bf16[512,384]{1,0:T(8,128)(2,1)S(1)} %copy-done.25, bf16[512,384]{1,0:T(8,128)(2,1)S(1)} %copy-done.27, ...), custom_call_target="tpu_custom_call", output_to_operand_aliasing={{0}: (11, {})} | custom-call | flops 10350000128 | bytes 10082304 | tf_op jit(solution)/shard_map/pallas_call | solution.py:43
  203.3 8.5 %collective-permute-done.25 = f32[2,2,48,768]{3,2,1,0:T(8,128)S(1)} collective-permute-done((f32[2,2,48,768]{3,2,1,0:T(8,128)S(1)}, f32[2,2,48,768]{3,2,1,0:T(8,128)S(1)}, u32[]{:S(2)}, u32[]{:S(2)}) %collective-permute-start.25) | collective-permute-done | bytes 589856 | tf_op jit(solution)/shard_map/ppermute | solution.py:395
  211.8 5.6 %collective-permute-done.26 = f32[2,2,48,1152]{3,2,1,0:T(8,128)S(1)} collective-permute-done((f32[2,2,48,1152]{3,2,1,0:T(8,128)S(1)}, f32[2,2,48,1152]{3,2,1,0:T(8,128)S(1)}, u32[]{:S(2)}, u32[]{:S(2)}) %collective-permute-start.26) | collective-permute-done | bytes 884768 | tf_op jit(solution)/shard_map/ppermute | solution.py:395
  222.7 5.5 %shard_map.328 = (f32[2,2,2,64,768]{4,3,2,1,0:T(8,128)S(1)}, f32[2,2,2,64,768]{4,3,2,1,0:T(8,128)}, f32[2,2,2,48,384]{4,3,2,1,0:T(8,128)S(1)}, f32[2,2,2,48,384]{4,3,2,1,0:T(8,128)S(1)}) custom-call(s32[1]{0:T(128)} %bitcast.8.core_ref, bf16[1024,768]{1,0:T(8,128)(2,1)} %x_ref.7, bf16[1024,1152]{1,0:T(8,128)(2,1)} %get-tuple-element.346.dqkv_ref, ...), custom_call_target="tpu_custom_call" | custom-call | flops 8049999872 | bytes 8429572 | tf_op jit(solution)/shard_map/pallas_call | solution.py:43
  228.2 14.6 %collective-permute-done.28 = f32[2,48,768]{2,1,0:T(8,128)S(1)} collective-permute-done((f32[2,48,768]{2,1,0:T(8,128)S(1)}, f32[2,48,768]{2,1,0:T(8,128)S(1)}, u32[]{:S(2)}, u32[]{:S(2)}) %collective-permute-start.28) | collective-permute-done | bytes 294944 | tf_op jit(solution)/shard_map/ppermute | solution.py:395
  252.6 4.8 %collective-permute-done.31 = f32[48,768]{1,0:T(8,128)S(1)} collective-permute-done((f32[48,768]{1,0:T(8,128)S(1)}, f32[48,768]{1,0:T(8,128)S(1)}, u32[]{:S(2)}, u32[]{:S(2)}) %collective-permute-start.31) | collective-permute-done | bytes 147488 | tf_op jit(solution)/shard_map/ppermute | solution.py:395
  257.3 10.2 %collective-permute-done.32 = f32[48,1152]{1,0:T(8,128)S(1)} collective-permute-done((f32[48,1152]{1,0:T(8,128)S(1)}, f32[48,1152]{1,0:T(8,128)S(1)}, u32[]{:S(2)}, u32[]{:S(2)}) %collective-permute-start.32) | collective-permute-done | bytes 221216 | tf_op jit(solution)/shard_map/ppermute | solution.py:395
  271.2 6.6 %collective-permute-done.37 = f32[2,2,48,384]{3,2,1,0:T(8,128)S(1)} collective-permute-done((f32[2,2,48,384]{3,2,1,0:T(8,128)S(1)}, f32[2,2,48,384]{3,2,1,0:T(8,128)S(1)}, u32[]{:S(2)}, u32[]{:S(2)}) %collective-permute-start.37) | collective-permute-done | bytes 294944 | tf_op jit(solution)/shard_map/ppermute | solution.py:395
  277.8 5.1 %collective-permute-done.36 = f32[2,2,64,768]{3,2,1,0:T(8,128)S(1)} collective-permute-done((f32[2,2,64,768]{3,2,1,0:T(8,128)S(1)}, f32[2,2,64,768]{3,2,1,0:T(8,128)S(1)}, u32[]{:S(2)}, u32[]{:S(2)}) %collective-permute-start.36) | collective-permute-done | bytes 786464 | tf_op jit(solution)/shard_map/ppermute | solution.py:395
  289.1 4.2 %collective-permute-start.40 = (f32[2,48,384]{2,1,0:T(8,128)S(1)}, f32[2,48,384]{2,1,0:T(8,128)S(1)}, u32[]{:S(2)}, u32[]{:S(2)}) collective-permute-start(f32[2,48,384]{2,1,0:T(8,128)S(1)} %get-tuple-element.459), channel_id=1, source_target_pairs={{0,16},{2,18},{4,20},{6,22},{8,24},{10,26},{12,28},{14,30},{16,0},... | collective-permute-start | bytes 442376 | tf_op jit(solution)/shard_map/ppermute | solution.py:395
  305.5 4.3 %collective-permute-done.42 = f32[64,768]{1,0:T(8,128)S(1)} collective-permute-done((f32[64,768]{1,0:T(8,128)S(1)}, f32[64,768]{1,0:T(8,128)S(1)}, u32[]{:S(2)}, u32[]{:S(2)}) %collective-permute-start.42) | collective-permute-done | bytes 196640 | tf_op jit(solution)/shard_map/ppermute | solution.py:395
  (240 shorter events, 103.2 us)
Async XLA Ops:
  7.2 109.2 %all-gather.2.cloned.1.call-start = ((), (), s32[]{:S(2)}) async-start(), calls=%async_computation.1 | async-start | bytes 5013504 | tf_op jit(solution)/shard_map/all_gather | solution.py:460
  13.8 19.6 %collective-permute-start.4 = (f32[48,1536]{1,0:T(8,128)}, f32[48,1536]{1,0:T(8,128)}, u32[]{:S(2)}, u32[]{:S(2)}) collective-permute-start(f32[48,1536]{1,0:T(8,128)} %convert_bitcast_fusion), channel_id=1, source_target_pairs={{0,1},{1,0},{2,3},{3,2},{4,5},{5,4},{6,7},{7,6},{8,9},{9,8},{10,11... | collective-permute-start | bytes 884744 | tf_op jit(solution)/shard_map/ppermute | solution.py:392
  16.2 17.3 %collective-permute-start.1 = (f32[96,384]{1,0:T(8,128)S(1)}, f32[96,384]{1,0:T(8,128)S(1)}, u32[]{:S(2)}, u32[]{:S(2)}) collective-permute-start(f32[96,384]{1,0:T(8,128)S(1)} %collective-permute-done.refs_0_), channel_id=1, source_target_pairs={{0,4},{2,6},{4,0},{6,2},{8,12},{10,14},{12,8},{14,10},{16,20},{18,... | collective-permute-start | bytes 442376 | tf_op jit(solution)/shard_map/ppermute | solution.py:395
  19.6 15.6 %collective-permute-start.3 = (f32[96,1536]{1,0:T(8,128)}, f32[96,1536]{1,0:T(8,128)}, u32[]{:S(2)}, u32[]{:S(2)}) collective-permute-start(f32[96,1536]{1,0:T(8,128)} %dynamic-slice_convert_fusion), channel_id=1, source_target_pairs={{0,1},{1,0},{2,3},{3,2},{4,5},{5,4},{6,7},{7,6},{8,9},{9,8},{10,11... | collective-permute-start | bytes 1769480 | tf_op jit(solution)/shard_map/ppermute | solution.py:392
  35.2 277.1 %reduce-scatter.2.cloned.1.call-start = ((), (), s32[]{:S(2)}) async-start(), calls=%async_computation.2 | async-start | bytes 5013504 | tf_op jit(solution)/shard_map/reduce_scatter | solution.py:579
  40.5 18.2 %collective-permute-start.6 = (f32[96,1536]{1,0:T(8,128)}, f32[96,1536]{1,0:T(8,128)S(1)}, u32[]{:S(2)}, u32[]{:S(2)}) collective-permute-start(f32[96,1536]{1,0:T(8,128)} %collective-permute-done.3.refs_0_), channel_id=1, source_target_pairs={{0,4},{2,6},{4,0},{6,2},{8,12},{10,14},{12,8},{14,10},{16,20},{18,... | collective-permute-start | bytes 1769480 | tf_op jit(solution)/shard_map/ppermute | solution.py:395
  41.6 23.9 %collective-permute-start.7 = (f32[96,1536]{1,0:T(8,128)}, f32[96,1536]{1,0:T(8,128)S(1)}, u32[]{:S(2)}, u32[]{:S(2)}) collective-permute-start(f32[96,1536]{1,0:T(8,128)} %collective-permute-done.3.refs_0_), channel_id=1, source_target_pairs={{0,8},{2,10},{4,12},{6,14},{8,0},{10,2},{12,4},{14,6},{16,24},{18,... | collective-permute-start | bytes 1769480 | tf_op jit(solution)/shard_map/ppermute | solution.py:395
  43.2 27.4 %collective-permute-start.16 = (f32[96,1536]{1,0:T(8,128)}, f32[96,1536]{1,0:T(8,128)S(1)}, u32[]{:S(2)}, u32[]{:S(2)}) collective-permute-start(f32[96,1536]{1,0:T(8,128)} %collective-permute-done.3.refs_0_), channel_id=1, source_target_pairs={{0,2},{2,0},{4,6},{6,4},{8,10},{10,8},{12,14},{14,12},{16,18},{18,... | collective-permute-start | bytes 1769480 | tf_op jit(solution)/shard_map/ppermute | solution.py:395
  43.7 21.8 %collective-permute-start.5 = (f32[520,384]{1,0:T(8,128)}, f32[520,384]{1,0:T(8,128)S(1)}, u32[]{:S(2)}, u32[]{:S(2)}) collective-permute-start(f32[520,384]{1,0:T(8,128)} %get-tuple-element.228), channel_id=1, source_target_pairs={{0,1},{1,0},{2,3},{3,2},{4,5},{5,4},{6,7},{7,6},{8,9},{9,8},{10,11... | collective-permute-start | bytes 2396168 | tf_op jit(solution)/shard_map/ppermute | solution.py:392
  66.1 24.5 %collective-permute-start.17 = (f32[96,1536]{1,0:T(8,128)S(1)}, f32[96,1536]{1,0:T(8,128)S(1)}, u32[]{:S(2)}, u32[]{:S(2)}) collective-permute-start(f32[96,1536]{1,0:T(8,128)S(1)} %collective-permute-done.6.refs_1_), channel_id=1, source_target_pairs={{0,2},{2,0},{4,6},{6,4},{8,10},{10,8},{12,14},{14,12},{16,18},{18,... | collective-permute-start | bytes 1769480 | tf_op jit(solution)/shard_map/ppermute | solution.py:395
  66.2 24.4 %collective-permute-start.18 = (f32[96,1536]{1,0:T(8,128)S(1)}, f32[96,1536]{1,0:T(8,128)S(1)}, u32[]{:S(2)}, u32[]{:S(2)}) collective-permute-start(f32[96,1536]{1,0:T(8,128)S(1)} %collective-permute-done.7.refs_2_), channel_id=1, source_target_pairs={{0,2},{2,0},{4,6},{6,4},{8,10},{10,8},{12,14},{14,12},{16,18},{18,... | collective-permute-start | bytes 1769480 | tf_op jit(solution)/shard_map/ppermute | solution.py:395
  66.7 23.9 %collective-permute-start.13 = (f32[512,384]{1,0:T(8,128)}, f32[512,384]{1,0:T(8,128)S(1)}, u32[]{:S(2)}, u32[]{:S(2)}) collective-permute-start(f32[512,384]{1,0:T(8,128)} %get-tuple-element.243), channel_id=1, source_target_pairs={{0,1},{1,0},{2,3},{3,2},{4,5},{5,4},{6,7},{7,6},{8,9},{9,8},{10,11... | collective-permute-start | bytes 2359304 | tf_op jit(solution)/shard_map/ppermute | solution.py:392
  70.5 20.0 %collective-permute-start.15 = (f32[48,1536]{1,0:T(8,128)S(1)}, f32[48,1536]{1,0:T(8,128)S(1)}, u32[]{:S(2)}, u32[]{:S(2)}) collective-permute-start(f32[48,1536]{1,0:T(8,128)S(1)} %slice.83), channel_id=1, source_target_pairs={{0,8},{2,10},{4,12},{6,14},{8,0},{10,2},{12,4},{14,6},{16,24},{18,... | collective-permute-start | bytes 884744 | tf_op jit(solution)/shard_map/ppermute | solution.py:395
  169.4 17.8 %collective-permute-start.24 = (f32[2,2,2,48,1152]{4,3,2,1,0:T(8,128)}, f32[2,2,2,48,1152]{4,3,2,1,0:T(8,128)}, u32[]{:S(2)}, u32[]{:S(2)}) collective-permute-start(f32[2,2,2,48,1152]{4,3,2,1,0:T(8,128)} %get-tuple-element.315), channel_id=1, source_target_pairs={{0,2},{2,0},{4,6},{6,4},{8,10},{10,8},{12,14},{14,12},{16,18},{18,... | collective-permute-start | bytes 5308424 | tf_op jit(solution)/shard_map/ppermute | solution.py:395
  189.0 28.4 %collective-permute-start.26 = (f32[2,2,48,1152]{3,2,1,0:T(8,128)S(1)}, f32[2,2,48,1152]{3,2,1,0:T(8,128)S(1)}, u32[]{:S(2)}, u32[]{:S(2)}) collective-permute-start(f32[2,2,48,1152]{3,2,1,0:T(8,128)S(1)} %get-tuple-element.431), channel_id=1, source_target_pairs={{0,4},{2,6},{4,0},{6,2},{8,12},{10,14},{12,8},{14,10},{16,20},{18,... | collective-permute-start | bytes 2654216 | tf_op jit(solution)/shard_map/ppermute | solution.py:395
  191.2 20.6 %collective-permute-start.25 = (f32[2,2,48,768]{3,2,1,0:T(8,128)S(1)}, f32[2,2,48,768]{3,2,1,0:T(8,128)S(1)}, u32[]{:S(2)}, u32[]{:S(2)}) collective-permute-start(f32[2,2,48,768]{3,2,1,0:T(8,128)S(1)} %get-tuple-element.437), channel_id=1, source_target_pairs={{0,8},{2,10},{4,12},{6,14},{8,0},{10,2},{12,4},{14,6},{16,24},{18,... | collective-permute-start | bytes 1769480 | tf_op jit(solution)/shard_map/ppermute | solution.py:395
  191.3 20.5 %collective-permute-start.27 = (f32[256,768]{1,0:T(8,128)S(1)}, f32[256,768]{1,0:T(8,128)S(1)}, u32[]{:S(2)}, u32[]{:S(2)}) collective-permute-start(f32[256,768]{1,0:T(8,128)S(1)} %copy-done.2), channel_id=1, source_target_pairs={{0,1},{1,0},{2,3},{3,2},{4,5},{5,4},{6,7},{7,6},{8,9},{9,8},{10,11... | collective-permute-start | bytes 2359304 | tf_op jit(solution)/shard_map/ppermute | solution.py:392
  217.6 27.1 %collective-permute-start.29 = (f32[2,48,1152]{2,1,0:T(8,128)S(1)}, f32[2,48,1152]{2,1,0:T(8,128)S(1)}, u32[]{:S(2)}, u32[]{:S(2)}) collective-permute-start(f32[2,48,1152]{2,1,0:T(8,128)S(1)} %get-tuple-element.439), channel_id=1, source_target_pairs={{0,8},{2,10},{4,12},{6,14},{8,0},{10,2},{12,4},{14,6},{16,24},{18,... | collective-permute-start | bytes 1327112 | tf_op jit(solution)/shard_map/ppermute | solution.py:395
  218.5 26.1 %collective-permute-start.30 = (f32[256,768]{1,0:T(8,128)S(1)}, f32[256,768]{1,0:T(8,128)S(1)}, u32[]{:S(2)}, u32[]{:S(2)}) collective-permute-start(f32[256,768]{1,0:T(8,128)S(1)} %copy-done.3), channel_id=1, source_target_pairs={{0,1},{1,0},{2,3},{3,2},{4,5},{5,4},{6,7},{7,6},{8,9},{9,8},{10,11... | collective-permute-start | bytes 2359304 | tf_op jit(solution)/shard_map/ppermute | solution.py:392
  220.7 22.1 %collective-permute-start.28 = (f32[2,48,768]{2,1,0:T(8,128)S(1)}, f32[2,48,768]{2,1,0:T(8,128)S(1)}, u32[]{:S(2)}, u32[]{:S(2)}) collective-permute-start(f32[2,48,768]{2,1,0:T(8,128)S(1)} %get-tuple-element.450), channel_id=1, source_target_pairs={{0,16},{2,18},{4,20},{6,22},{8,24},{10,26},{12,28},{14,30},{16,0},... | collective-permute-start | bytes 884744 | tf_op jit(solution)/shard_map/ppermute | solution.py:395
  244.7 22.9 %collective-permute-start.33 = (f32[2,2,2,64,768]{4,3,2,1,0:T(8,128)}, f32[2,2,2,64,768]{4,3,2,1,0:T(8,128)S(1)}, u32[]{:S(2)}, u32[]{:S(2)}) collective-permute-start(f32[2,2,2,64,768]{4,3,2,1,0:T(8,128)} %get-tuple-element.370), channel_id=1, source_target_pairs={{0,2},{2,0},{4,6},{6,4},{8,10},{10,8},{12,14},{14,12},{16,18},{18,... | collective-permute-start | bytes 4718600 | tf_op jit(solution)/shard_map/ppermute | solution.py:395
  244.7 22.9 %collective-permute-start.34 = (f32[2,2,2,48,384]{4,3,2,1,0:T(8,128)S(1)}, f32[2,2,2,48,384]{4,3,2,1,0:T(8,128)S(1)}, u32[]{:S(2)}, u32[]{:S(2)}) collective-permute-start(f32[2,2,2,48,384]{4,3,2,1,0:T(8,128)S(1)} %get-tuple-element.372), channel_id=1, source_target_pairs={{0,2},{2,0},{4,6},{6,4},{8,10},{10,8},{12,14},{14,12},{16,18},{18,... | collective-permute-start | bytes 1769480 | tf_op jit(solution)/shard_map/ppermute | solution.py:395
  245.3 22.2 %collective-permute-start.32 = (f32[48,1152]{1,0:T(8,128)S(1)}, f32[48,1152]{1,0:T(8,128)S(1)}, u32[]{:S(2)}, u32[]{:S(2)}) collective-permute-start(f32[48,1152]{1,0:T(8,128)S(1)} %get-tuple-element.454), channel_id=1, source_target_pairs={{0,16},{2,18},{4,20},{6,22},{8,24},{10,26},{12,28},{14,30},{16,0},... | collective-permute-start | bytes 663560 | tf_op jit(solution)/shard_map/ppermute | solution.py:395
  246.9 20.7 %collective-permute-start.35 = (f32[128,768]{1,0:T(8,128)S(1)}, f32[128,768]{1,0:T(8,128)S(1)}, u32[]{:S(2)}, u32[]{:S(2)}) collective-permute-start(f32[128,768]{1,0:T(8,128)S(1)} %get-tuple-element.395.refs_0_), channel_id=1, source_target_pairs={{0,1},{1,0},{2,3},{3,2},{4,5},{5,4},{6,7},{7,6},{8,9},{9,8},{10,11... | collective-permute-start | bytes 1179656 | tf_op jit(solution)/shard_map/ppermute | solution.py:392
  (72 other events, 598.9 us)
Sparse Core Ops, SparseCore 0:
  35.4 65.2 all-gather.1
  172.5 96.2 reduce-scatter.1
where the time goes:
time: 324 us; the launch traced here: 319 us
  Pallas kernels  132 us (41%)
  waiting for transfers between devices  89.5 us (28%)
  starting transfers between devices  48.5 us (15%)
  local copies, waits for them, and re-layouts  25.6 us (8%)
  between operations  15.1 us (5%)
  other arithmetic  8.86 us (3%)
    pallas_call x17, Pallas kernels, call(): pl.pallas_call(body, grid=grid, in_specs=[spec(a.shape, b, i) for a, b, i...  132 us
    ppermute x34, waiting for transfers between devices, swap_dp(): return lax.ppermute(array, 'dp', [(i, i ^ bit) for i in range(dp)])  86.4 us
    ppermute x34, starting transfers between devices, swap_dp(): return lax.ppermute(array, 'dp', [(i, i ^ bit) for i in range(dp)])  31.8 us
    unnamed x102, local copies, waits for them, and re-layouts  16.4 us
    ppermute x10, starting transfers between devices, swap_mp(): return lax.ppermute(array, 'mp', [(0, 1), (1, 0)])  16.1 us
  transfers between devices with their start and end apart: 46, of which 20 were waited for; matrix products, arithmetic and copies ran while one was open for 5% of the time, Pallas kernels for 26%

commit v1 on v0

--- a/solution.py
+++ b/solution.py
@@ -13,6 +13,8 @@
 QUERY_CHUNK = 256
 UNIT_BLOCK = 512
 BACK_BLOCK = 256
+UP_ORDERS = ("lux", "xlu")
+LAST_ORDERS = ("xlu", "lux")
 norm_eps = 1e-05
 masked_value = -1000000000.0
 BF = jnp.bfloat16
@@ -280,26 +282,24 @@
         at += mine_ref.shape[0]
 
 
-def scatter_rows(g, first, keep_ref, send_ref, rows, extra=None):
-    over, across = keep_ref.shape[1:3]
-    for block in range(keep_ref.shape[0] * over * across):
+def put(g, core_ref, outs, rows, order, extra=None):
+    if len(outs) == 1:
+        outs[0][:g.shape[0]] = g
+        if extra is not None:
+            outs[0][g.shape[0]:] = extra
+        return
+    keep_ref, send_ref = outs
+    first = core_ref[0] == 0
+    for block in range(8):
         at = 2 * block * rows
         even, odd = g[at:at + rows], g[at + rows:at + 2 * rows]
-        place = (block // (over * across), block // across % over, block % across)
+        bits = {"u": block // 4, "l": block // 2 % 2, "x": block % 2}
+        place = tuple(bits[stage] for stage in order)
         keep_ref[place + (slice(0, rows),)] = jnp.where(first, even, odd)
         send_ref[place + (slice(0, rows),)] = jnp.where(first, odd, even)
         if extra is not None:
             keep_ref[place + (slice(rows, None),)] = extra
             send_ref[place + (slice(rows, None),)] = extra
-
-
-def put(g, core_ref, outs, rows, extra=None):
-    if len(outs) == 2:
-        scatter_rows(g, core_ref[0] == 0, *outs, rows, extra)
-    else:
-        outs[0][:g.shape[0]] = g
-        if extra is not None:
-            outs[0][g.shape[0]:] = extra
 
 
 def turn(refs, turned, step=0):
@@ -326,16 +326,16 @@
 
     @pl.when(pl.program_id(0) < last // 2)
     def _():
-        put(nn(turned[...], right_ref[...]), core_ref, outs[:count], rows)
+        put(nn(turned[...], right_ref[...]), core_ref, outs[:count], rows, UP_ORDERS[0])
 
     @pl.when((pl.program_id(0) >= last // 2) & (pl.program_id(0) < last))
     def _():
-        put(nn(turned[...], right_ref[...]), core_ref, outs[count:], rows)
+        put(nn(turned[...], right_ref[...]), core_ref, outs[count:], rows, UP_ORDERS[1])
 
     @pl.when(pl.program_id(0) == last)
     def _():
         g = nn(turned[:, :length], ca_ref[...]) + nn(turned[:, length:], cb_ref[...])
-        put(g, core_ref, outs[count:], rows)
+        put(g, core_ref, outs[count:], rows, UP_ORDERS[1])
 
 
 def gradient_attention(
@@ -353,8 +353,8 @@
     pieces.append(jnp.zeros((-have % 16, width), F32))
     extra = jnp.concatenate(pieces, axis=0)
     turn((x_ref,), turned)
-    put(nn(turned[...], dqkv_ref[:, :2 * half]), core_ref, outs[:count], rows, extra)
-    put(nn(turned[...], dqkv_ref[:, 2 * half:]), core_ref, outs[count:], rows)
+    put(nn(turned[...], dqkv_ref[:, :2 * half]), core_ref, outs[:count], rows, LAST_ORDERS[0], extra)
+    put(nn(turned[...], dqkv_ref[:, 2 * half:]), core_ref, outs[count:], rows, LAST_ORDERS[1])
 
 
 def join_pieces(place_ref, *refs):
@@ -527,7 +527,7 @@
 
     split = dp == 16
     core_arg = jnp.reshape(core, (1,)).astype(jnp.int32)
-    lead = (2, dp // 8, 2, width // dp)
+    lead = (2, 2, 2, width // dp)
     turned = pltpu.VMEM((width, tokens), BF)
 
     def parted(cols, block, index, extra=0):
@@ -545,7 +545,6 @@
 
     class Reduction:
         def __init__(self, parts, order, terms=None):
-            self.names = ["u", "l", "x"]
             self.order, self.parts, self.terms = list(order), parts, terms
 
         def step(self):
@@ -556,12 +555,10 @@
                 self.terms = [self.parts[0], got]
                 return got
             stage = self.order.pop(0)
-            axis = self.names.index(stage)
-            self.names.pop(axis)
             bit = bits[stage]
-            send = sum(pick(term, 1 - bit, axis) for term in self.terms)
+            send = sum(pick(term, 1 - bit, 0) for term in self.terms)
             got = swap_dp(send, hops[stage])
-            self.terms = [pick(term, bit, axis) for term in self.terms] + [got]
+            self.terms = [pick(term, bit, 0) for term in self.terms] + [got]
             return got
 
         def result(self):
@@ -612,7 +609,7 @@
         [turned], 9.0,
     )
     up, d_context = lock(up, d_context)
-    up = [Reduction(parts, order) for parts, order in zip(pairs(up), ("lux", "xlu"))]
+    up = [Reduction(parts, order) for parts, order in zip(pairs(up), UP_ORDERS)]
 
     def advance(reductions, *values):
         for one in reductions:
@@ -637,8 +634,8 @@
         parted(2 * half, 2 * half, lambda i: 0, 16) + parted(half, half, lambda i: 0),
         [turned], 7.0,
     )
-    last, mine_b, theirs_a = advance(up, last, mine_b, theirs_a)
-    query, value = [Reduction(parts, order) for parts, order in zip(pairs(last), ("xlu", "lux"))]
+    last, mine_b, theirs_a, down_part = advance(up, last, mine_b, theirs_a, down_part)
+    query, value = [Reduction(parts, order) for parts, order in zip(pairs(last), LAST_ORDERS)]
     theirs_b = []
     for moving in (up + [query, value], [query, value], [query, value]):
         theirs_b.append(swap_mp(mine_b[len(theirs_b)]))

time: 324 us -> 307 us (0.948)
  waiting for transfers between devices: 89.5 us -> 68.5 us
    ppermute x34, waiting for transfers between devices: 86.4 us -> 65.2 us  [swap_dp(): return lax.ppermute(array, 'dp', [(i, i ^ bit) for i in range(dp)])]
    unnamed x102 -> x144, local copies, waits for them, and re-layouts: 16.4 us -> 17.7 us
  transfers between devices with their start and end apart: 46 -> 46, of which waited for: 20 -> 22; matrix products, arithmetic and copies ran while one was open for 5% -> 5% of each run, Pallas kernels for 26% -> 38%
where the time goes in v1:
time: 307 us; the launch traced here: 302 us
  Pallas kernels  132 us (43%)
  waiting for transfers between devices  68.5 us (22%)
  starting transfers between devices  49.3 us (16%)
  local copies, waits for them, and re-layouts  25.3 us (8%)
  between operations  15.2 us (5%)
  other arithmetic  12 us (4%)
    pallas_call x17, Pallas kernels, call(): pl.pallas_call(body, grid=grid, in_specs=[spec(a.shape, b, i) for a, b, i...  132 us
    ppermute x34, waiting for transfers between devices, swap_dp(): return lax.ppermute(array, 'dp', [(i, i ^ bit) for i in range(dp)])  65.2 us
    ppermute x34, starting transfers between devices, swap_dp(): return lax.ppermute(array, 'dp', [(i, i ^ bit) for i in range(dp)])  34.3 us
    unnamed x144, local copies, waits for them, and re-layouts  17.7 us
    ppermute x10, starting transfers between devices, swap_mp(): return lax.ppermute(array, 'mp', [(0, 1), (1, 0)])  14.4 us
    add x12, other arithmetic, step(): send = sum((pick(term, 1 - bit, 0) for term in self.terms))  7.83 us
  transfers between devices with their start and end apart: 46, of which 22 were waited for; matrix products, arithmetic and copies ran while one was open for 5% of the time, Pallas kernels for 38%

profile of v1, /device:TPU:0, one launch (start us, length us, event | category | flops | bytes accessed | tf_op | source)
XLA Modules:
  0.0 302.4 jit_solution(5424760947901790855)
XLA Ops:
  21.3 10.0 %shard_map.314 = (bf16[512,384]{1,0:T(8,128)(2,1)S(1)}, bf16[512,384]{1,0:T(8,128)(2,1)S(1)}, bf16[512,384]{1,0:T(8,128)(2,1)S(1)}, bf16[512,384]{1,0:T(8,128)(2...) custom-call(bf16[1024,768]{1,0:T(8,128)(2,1)} %x_ref.7, bf16[768,384]{1,0:T(8,128)(2,1)S(1)} %copy-done.10, ...), custom_call_target="tpu_custom_call" | custom-call | flops 10350000128 | bytes 5741568 | tf_op jit(solution)/shard_map/pallas_call | solution.py:45
  46.5 9.9 %shard_map.315 = (bf16[512,384]{1,0:T(8,128)(2,1)S(1)}, bf16[512,384]{1,0:T(8,128)(2,1)S(1)}, bf16[512,384]{1,0:T(8,128)(2,1)S(1)}, bf16[512,384]{1,0:T(8,128)(2...) custom-call(bf16[1024,768]{1,0:T(8,128)(2,1)} %x_ref.7, bf16[768,384]{1,0:T(8,128)(2,1)S(1)} %copy-done.10, ...), custom_call_target="tpu_custom_call" | custom-call | flops 10350000128 | bytes 5729280 | tf_op jit(solution)/shard_map/pallas_call | solution.py:45
  59.4 6.6 %collective-permute-done.7.refs_2_ = f32[96,1536]{1,0:T(8,128)S(1)} collective-permute-done((f32[96,1536]{1,0:T(8,128)}, f32[96,1536]{1,0:T(8,128)S(1)}, u32[]{:S(2)}, u32[]{:S(2)}) %collective-permute-start.7) | collective-permute-done | bytes 589856 | tf_op jit(solution)/shard_map/ppermute | solution.py:395
  72.4 8.8 %shard_map.317 = (bf16[512,768]{1,0:T(8,128)(2,1)S(1)}, f32[512,768]{1,0:T(8,128)}, f32[1024,768]{1,0:T(8,128)}, bf16[1024,1536]{1,0:T(8,128)(2,1)}, bf16[1024,1536]{1,0:T(8,128)(2,1)}) custom-call(bf16[1024,768]{1,0:T(8,128)(2,1)} %x_ref.7, bf16[512,384]{1,0:T(8,128)(2,1)S(1)} %copy-done.32, f32[520,384]{1,0:T(8,128)S(1)} %collective-permute-done.5.cx_ref.bu_ref, ...), custom_call_target="tpu_custom_call" | custom-call | flops 9200000000 | bytes 20477952 | tf_op jit(solution)/shard_map/pallas_call | solution.py:45
  82.9 8.0 %collective-permute-done.15.refs_4_ = f32[48,1536]{1,0:T(8,128)S(1)} collective-permute-done((f32[48,1536]{1,0:T(8,128)S(1)}, f32[48,1536]{1,0:T(8,128)S(1)}, u32[]{:S(2)}, u32[]{:S(2)}) %collective-permute-start.15) | collective-permute-done | bytes 294944 | tf_op jit(solution)/shard_map/ppermute | solution.py:395
  93.1 3.0 %shard_map.319.wu_ref.wux_ref = bf16[768,1536]{1,0:T(8,128)(2,1)} custom-call(s32[2]{0:T(128)S(1)} %pad_add_fusion.place_ref, f32[96,1536]{1,0:T(8,128)} %collective-permute-done.3.refs_0_, f32[96,1536]{1,0:T(8,128)S(1)} %collective-permute-done.6.refs_1_, f32[96,1536]{1,0:T(8,128)S(1)} %collective-permute-done.7.refs_2_, ...), custom_call_target="tpu_custom_call" | custom-call | flops 3449999872 | bytes 7077896 | tf_op jit(solution)/shard_map/pallas_call | solution.py:45
  97.9 4.6 %shard_map.320 = (bf16[1024,1536]{1,0:T(8,128)(2,1)}, bf16[1024,1536]{1,0:T(8,128)(2,1)}) custom-call(bf16[512,768]{1,0:T(8,128)(2,1)S(1)} %get-tuple-element.289.nlow_ref.la_ref, bf16[768,1536]{1,0:T(8,128)(2,1)S(1)} %copy-done.19, f32[520,384]{1,0:T(8,128)S(1)} %collective-permute-done.5.cx_ref.bu_ref), custom_call_target="tpu_custom_call" | custom-call | flops 4600000000 | bytes 10235904 | tf_op jit(solution)/shard_map/pallas_call | solution.py:45
  102.5 8.6 %shard_map.318 = (bf16[512,768]{1,0:T(8,128)(2,1)S(1)}, f32[512,768]{1,0:T(8,128)}, f32[1024,768]{1,0:T(8,128)}, bf16[1024,1536]{1,0:T(8,128)(2,1)}, bf16[1024,1536]{1,0:T(8,128)(2,1)}) custom-call(bf16[1024,768]{1,0:T(8,128)(2,1)} %x_ref.7, ...), custom_call_target="tpu_custom_call", output_to_operand_aliasing={{2}: (12, {}), {3}: (13, {}), {4}: (14, {})} | custom-call | flops 9200000000 | bytes 29902848 | tf_op jit(solution)/shard_map/pallas_call | solution.py:45
  111.1 4.8 %shard_map.321 = (bf16[1024,1536]{1,0:T(8,128)(2,1)}, bf16[1024,1536]{1,0:T(8,128)(2,1)}) custom-call(bf16[512,768]{1,0:T(8,128)(2,1)S(1)} %get-tuple-element.278.nlow_ref.lb_ref, bf16[768,1536]{1,0:T(8,128)(2,1)S(1)} %copy-done.20, f32[520,384]{1,0:T(8,128)S(1)} %collective-permute-done.5.cx_ref.bu_ref, ...), custom_call_target="tpu_custom_call", output_to_operand_aliasing={{0}: (3, {}), {1}: (4, {})} | custom-call | flops 4600000000 | bytes 16527360 | tf_op jit(solution)/shard_map/pallas_call | solution.py:45
  117.4 11.4 %shard_map.322 = (bf16[1024,768]{1,0:T(8,128)(2,1)}, f32[1024,768]{1,0:T(8,128)}, bf16[1024,768]{1,0:T(8,128)(2,1)S(1)}, f32[8,768]{1,0:T(8,128)S(1)}, bf16[768,1536]{1,0:T(8,128)(2,1)}) custom-call(bf16[1024,1536]{1,0:T(8,128)(2,1)} %get-tuple-element.292.act_ref, f32[512,768]{1,0:T(8,128)S(1)} %copy-done.26, f32[512,768]{1,0:T(8,128)} %get-tuple-element.294.startb_ref, ...), custom_call_target="tpu_custom_call" | custom-call | flops 11500000256 | bytes 21264384 | tf_op jit(solution)/shard_map/pallas_call | solution.py:45
  128.8 6.8 %shard_map.323 = f32[768,1536]{1,0:T(8,128)} custom-call(bf16[1024,768]{1,0:T(8,128)(2,1)S(1)} %get-tuple-element.299.left_ref.dffn_ref, bf16[1024,1536]{1,0:T(8,128)(2,1)} %get-tuple-element.298.right_ref), custom_call_target="tpu_custom_call" | custom-call | flops 6899999744 | bytes 9437184 | tf_op jit(solution)/shard_map/pallas_call | solution.py:45
  136.9 20.8 %shard_map.324 = (bf16[1024,1536]{1,0:T(8,128)(2,1)}, f32[8,1536]{1,0:T(8,128)S(1)}, f32[1024,768]{1,0:T(8,128)}, bf16[1024,768]{1,0:T(8,128)(2,1)S(1)}, bf16[10...) custom-call(bf16[1024,768]{1,0:T(8,128)(2,1)} %copy-done.23, bf16[1024,1536]{1,0:T(8,128)(2,1)} %get-tuple-element.300.so_ref, ...), custom_call_target="tpu_custom_call" | custom-call | flops 23000000512 | bytes 32910336 | tf_op jit(solution)/shard_map/pallas_call | solution.py:45
  159.8 9.7 %shard_map.325 = (f32[2,2,2,48,768]{4,3,2,1,0:T(8,128)S(1)}, f32[2,2,2,48,768]{4,3,2,1,0:T(8,128)}, f32[2,2,2,48,1152]{4,3,2,1,0:T(8,128)}, f32[2,2,2,48,1152]{4,3,2,1,0:T(8,128)}) custom-call(s32[1]{0:T(128)} %bitcast.8.core_ref, bf16[512,768]{1,0:T(8,128)(2,1)S(1)} %copy-done.25, bf16[512,768]{1,0:T(8,128)(2,1)S(1)} %copy-done.22, ...), custom_call_target="tpu_custom_call" | custom-call | flops 10350000128 | bytes 12976132 | tf_op jit(solution)/shard_map/pallas_call | solution.py:45
  175.2 10.7 %shard_map.326 = (bf16[1024,1152]{1,0:T(8,128)(2,1)}, f32[8,1152]{1,0:T(8,128)S(1)}, f32[256,768]{1,0:T(8,128)}, f32[256,768]{1,0:T(8,128)}) custom-call(bf16[512,384]{1,0:T(8,128)(2,1)S(1)} %copy-done.41, bf16[512,384]{1,0:T(8,128)(2,1)S(1)} %copy-done.43, bf16[512,384]{1,0:T(8,128)(2,1)S(1)} %copy-done.45, f32[6,512]{1,0:T(8,128)S(1)} %get-tuple-element.320.lse_ref, ...), custom_call_target="tpu_custom_call" | custom-call | flops 10350000128 | bytes 7723008 | tf_op jit(solution)/shard_map/pallas_call | solution.py:45
  191.5 10.7 %shard_map.327 = (bf16[1024,1152]{1,0:T(8,128)(2,1)}, f32[8,1152]{1,0:T(8,128)S(1)}, f32[128,768]{1,0:T(8,128)S(1)}, f32[256,768]{1,0:T(8,128)}, f32[128,768]{1,0:T(8,128)S(1)}) custom-call(bf16[512,384]{1,0:T(8,128)(2,1)S(1)} %copy-done.35, bf16[512,384]{1,0:T(8,128)(2,1)S(1)} %copy-done.37, ...), custom_call_target="tpu_custom_call", output_to_operand_aliasing={{0}: (11, {})} | custom-call | flops 10350000128 | bytes 10082304 | tf_op jit(solution)/shard_map/pallas_call | solution.py:45
  202.2 10.3 %collective-permute-done.25 = f32[2,2,48,768]{3,2,1,0:T(8,128)S(1)} collective-permute-done((f32[2,2,48,768]{3,2,1,0:T(8,128)S(1)}, f32[2,2,48,768]{3,2,1,0:T(8,128)S(1)}, u32[]{:S(2)}, u32[]{:S(2)}) %collective-permute-start.25) | collective-permute-done | bytes 589856 | tf_op jit(solution)/shard_map/ppermute | solution.py:395
  216.5 6.2 %collective-permute-start.28 = (f32[2,48,768]{2,1,0:T(8,128)S(1)}, f32[2,48,768]{2,1,0:T(8,128)S(1)}, u32[]{:S(2)}, u32[]{:S(2)}) collective-permute-start(f32[2,48,768]{2,1,0:T(8,128)S(1)} %get-tuple-element.453), channel_id=1, source_target_pairs={{0,16},{2,18},{4,20},{6,22},{8,24},{10,26},{12,28},{14,30},{16,0},... | collective-permute-start | bytes 884744 | tf_op jit(solution)/shard_map/ppermute | solution.py:395
  222.7 5.5 %shard_map.328 = (f32[2,2,2,64,768]{4,3,2,1,0:T(8,128)S(1)}, f32[2,2,2,64,768]{4,3,2,1,0:T(8,128)}, f32[2,2,2,48,384]{4,3,2,1,0:T(8,128)S(1)}, f32[2,2,2,48,384]{4,3,2,1,0:T(8,128)S(1)}) custom-call(s32[1]{0:T(128)} %bitcast.8.core_ref, bf16[1024,768]{1,0:T(8,128)(2,1)} %x_ref.7, bf16[1024,1152]{1,0:T(8,128)(2,1)} %get-tuple-element.347.dqkv_ref, ...), custom_call_target="tpu_custom_call" | custom-call | flops 8049999872 | bytes 8429572 | tf_op jit(solution)/shard_map/pallas_call | solution.py:45
  236.2 3.6 %collective-permute-start.32 = (f32[48,1152]{1,0:T(8,128)S(1)}, f32[48,1152]{1,0:T(8,128)S(1)}, u32[]{:S(2)}, u32[]{:S(2)}) collective-permute-start(f32[48,1152]{1,0:T(8,128)S(1)} %get-tuple-element.457), channel_id=1, source_target_pairs={{0,16},{2,18},{4,20},{6,22},{8,24},{10,26},{12,28},{14,30},{16,0},... | collective-permute-start | bytes 663560 | tf_op jit(solution)/shard_map/ppermute | solution.py:395
  246.6 3.3 %collective-permute-done.32 = f32[48,1152]{1,0:T(8,128)S(1)} collective-permute-done((f32[48,1152]{1,0:T(8,128)S(1)}, f32[48,1152]{1,0:T(8,128)S(1)}, u32[]{:S(2)}, u32[]{:S(2)}) %collective-permute-start.32) | collective-permute-done | bytes 221216 | tf_op jit(solution)/shard_map/ppermute | solution.py:395
  254.2 7.2 %collective-permute-done.37 = f32[2,2,48,384]{3,2,1,0:T(8,128)S(1)} collective-permute-done((f32[2,2,48,384]{3,2,1,0:T(8,128)S(1)}, f32[2,2,48,384]{3,2,1,0:T(8,128)S(1)}, u32[]{:S(2)}, u32[]{:S(2)}) %collective-permute-start.37) | collective-permute-done | bytes 294944 | tf_op jit(solution)/shard_map/ppermute | solution.py:395
  261.4 8.1 %collective-permute-done.36 = f32[2,2,64,768]{3,2,1,0:T(8,128)S(1)} collective-permute-done((f32[2,2,64,768]{3,2,1,0:T(8,128)S(1)}, f32[2,2,64,768]{3,2,1,0:T(8,128)S(1)}, u32[]{:S(2)}, u32[]{:S(2)}) %collective-permute-start.36) | collective-permute-done | bytes 786464 | tf_op jit(solution)/shard_map/ppermute | solution.py:395
  275.9 4.9 %collective-permute-done.40 = f32[2,48,384]{2,1,0:T(8,128)S(1)} collective-permute-done((f32[2,48,384]{2,1,0:T(8,128)S(1)}, f32[2,48,384]{2,1,0:T(8,128)S(1)}, u32[]{:S(2)}, u32[]{:S(2)}) %collective-permute-start.40) | collective-permute-done | bytes 147488 | tf_op jit(solution)/shard_map/ppermute | solution.py:395
  289.2 3.5 %collective-permute-done.42 = f32[64,768]{1,0:T(8,128)S(1)} collective-permute-done((f32[64,768]{1,0:T(8,128)S(1)}, f32[64,768]{1,0:T(8,128)S(1)}, u32[]{:S(2)}, u32[]{:S(2)}) %collective-permute-start.42) | collective-permute-done | bytes 196640 | tf_op jit(solution)/shard_map/ppermute | solution.py:395
  (280 shorter events, 99.9 us)
Async XLA Ops:
  7.3 108.7 %all-gather.2.cloned.1.call-start = ((), (), s32[]{:S(2)}) async-start(), calls=%async_computation.1 | async-start | bytes 5013504 | tf_op jit(solution)/shard_map/all_gather | solution.py:460
  13.9 20.4 %collective-permute-start.4 = (f32[48,1536]{1,0:T(8,128)}, f32[48,1536]{1,0:T(8,128)}, u32[]{:S(2)}, u32[]{:S(2)}) collective-permute-start(f32[48,1536]{1,0:T(8,128)} %convert_bitcast_fusion), channel_id=1, source_target_pairs={{0,1},{1,0},{2,3},{3,2},{4,5},{5,4},{6,7},{7,6},{8,9},{9,8},{10,11... | collective-permute-start | bytes 884744 | tf_op jit(solution)/shard_map/ppermute | solution.py:392
  16.2 18.1 %collective-permute-start.1 = (f32[96,384]{1,0:T(8,128)S(1)}, f32[96,384]{1,0:T(8,128)S(1)}, u32[]{:S(2)}, u32[]{:S(2)}) collective-permute-start(f32[96,384]{1,0:T(8,128)S(1)} %collective-permute-done.refs_0_), channel_id=1, source_target_pairs={{0,4},{2,6},{4,0},{6,2},{8,12},{10,14},{12,8},{14,10},{16,20},{18,... | collective-permute-start | bytes 442376 | tf_op jit(solution)/shard_map/ppermute | solution.py:395
  18.1 16.1 %collective-permute-start.2 = (f32[96,384]{1,0:T(8,128)S(1)}, f32[96,384]{1,0:T(8,128)S(1)}, u32[]{:S(2)}, u32[]{:S(2)}) collective-permute-start(f32[96,384]{1,0:T(8,128)S(1)} %collective-permute-done.refs_0_), channel_id=1, source_target_pairs={{0,8},{2,10},{4,12},{6,14},{8,0},{10,2},{12,4},{14,6},{16,24},{18,... | collective-permute-start | bytes 442376 | tf_op jit(solution)/shard_map/ppermute | solution.py:395
  35.3 198.3 %reduce-scatter.2.cloned.1.call-start = ((), (), s32[]{:S(2)}) async-start(), calls=%async_computation.2 | async-start | bytes 5013504 | tf_op jit(solution)/shard_map/reduce_scatter | solution.py:576
  41.2 18.2 %collective-permute-start.6 = (f32[96,1536]{1,0:T(8,128)}, f32[96,1536]{1,0:T(8,128)S(1)}, u32[]{:S(2)}, u32[]{:S(2)}) collective-permute-start(f32[96,1536]{1,0:T(8,128)} %collective-permute-done.3.refs_0_), channel_id=1, source_target_pairs={{0,4},{2,6},{4,0},{6,2},{8,12},{10,14},{12,8},{14,10},{16,20},{18,... | collective-permute-start | bytes 1769480 | tf_op jit(solution)/shard_map/ppermute | solution.py:395
  41.8 24.2 %collective-permute-start.7 = (f32[96,1536]{1,0:T(8,128)}, f32[96,1536]{1,0:T(8,128)S(1)}, u32[]{:S(2)}, u32[]{:S(2)}) collective-permute-start(f32[96,1536]{1,0:T(8,128)} %collective-permute-done.3.refs_0_), channel_id=1, source_target_pairs={{0,8},{2,10},{4,12},{6,14},{8,0},{10,2},{12,4},{14,6},{16,24},{18,... | collective-permute-start | bytes 1769480 | tf_op jit(solution)/shard_map/ppermute | solution.py:395
  43.9 27.3 %collective-permute-start.16 = (f32[96,1536]{1,0:T(8,128)}, f32[96,1536]{1,0:T(8,128)S(1)}, u32[]{:S(2)}, u32[]{:S(2)}) collective-permute-start(f32[96,1536]{1,0:T(8,128)} %collective-permute-done.3.refs_0_), channel_id=1, source_target_pairs={{0,2},{2,0},{4,6},{6,4},{8,10},{10,8},{12,14},{14,12},{16,18},{18,... | collective-permute-start | bytes 1769480 | tf_op jit(solution)/shard_map/ppermute | solution.py:395
  44.4 21.6 %collective-permute-start.5 = (f32[520,384]{1,0:T(8,128)}, f32[520,384]{1,0:T(8,128)S(1)}, u32[]{:S(2)}, u32[]{:S(2)}) collective-permute-start(f32[520,384]{1,0:T(8,128)} %get-tuple-element.229), channel_id=1, source_target_pairs={{0,1},{1,0},{2,3},{3,2},{4,5},{5,4},{6,7},{7,6},{8,9},{9,8},{10,11... | collective-permute-start | bytes 2396168 | tf_op jit(solution)/shard_map/ppermute | solution.py:392
  66.6 24.4 %collective-permute-start.17 = (f32[96,1536]{1,0:T(8,128)S(1)}, f32[96,1536]{1,0:T(8,128)S(1)}, u32[]{:S(2)}, u32[]{:S(2)}) collective-permute-start(f32[96,1536]{1,0:T(8,128)S(1)} %collective-permute-done.6.refs_1_), channel_id=1, source_target_pairs={{0,2},{2,0},{4,6},{6,4},{8,10},{10,8},{12,14},{14,12},{16,18},{18,... | collective-permute-start | bytes 1769480 | tf_op jit(solution)/shard_map/ppermute | solution.py:395
  66.7 24.2 %collective-permute-start.18 = (f32[96,1536]{1,0:T(8,128)S(1)}, f32[96,1536]{1,0:T(8,128)S(1)}, u32[]{:S(2)}, u32[]{:S(2)}) collective-permute-start(f32[96,1536]{1,0:T(8,128)S(1)} %collective-permute-done.7.refs_2_), channel_id=1, source_target_pairs={{0,2},{2,0},{4,6},{6,4},{8,10},{10,8},{12,14},{14,12},{16,18},{18,... | collective-permute-start | bytes 1769480 | tf_op jit(solution)/shard_map/ppermute | solution.py:395
  67.5 23.5 %collective-permute-start.13 = (f32[512,384]{1,0:T(8,128)}, f32[512,384]{1,0:T(8,128)S(1)}, u32[]{:S(2)}, u32[]{:S(2)}) collective-permute-start(f32[512,384]{1,0:T(8,128)} %get-tuple-element.244), channel_id=1, source_target_pairs={{0,1},{1,0},{2,3},{3,2},{4,5},{5,4},{6,7},{7,6},{8,9},{9,8},{10,11... | collective-permute-start | bytes 2359304 | tf_op jit(solution)/shard_map/ppermute | solution.py:392
  71.2 19.8 %collective-permute-start.15 = (f32[48,1536]{1,0:T(8,128)S(1)}, f32[48,1536]{1,0:T(8,128)S(1)}, u32[]{:S(2)}, u32[]{:S(2)}) collective-permute-start(f32[48,1536]{1,0:T(8,128)S(1)} %slice.83), channel_id=1, source_target_pairs={{0,8},{2,10},{4,12},{6,14},{8,0},{10,2},{12,4},{14,6},{16,24},{18,... | collective-permute-start | bytes 884744 | tf_op jit(solution)/shard_map/ppermute | solution.py:395
  169.5 16.4 %collective-permute-start.24 = (f32[2,2,2,48,1152]{4,3,2,1,0:T(8,128)}, f32[2,2,2,48,1152]{4,3,2,1,0:T(8,128)}, u32[]{:S(2)}, u32[]{:S(2)}) collective-permute-start(f32[2,2,2,48,1152]{4,3,2,1,0:T(8,128)} %get-tuple-element.316), channel_id=1, source_target_pairs={{0,2},{2,0},{4,6},{6,4},{8,10},{10,8},{12,14},{14,12},{16,18},{18,... | collective-permute-start | bytes 5308424 | tf_op jit(solution)/shard_map/ppermute | solution.py:395
  169.6 16.2 %collective-permute-start.23 = (f32[2,2,2,48,768]{4,3,2,1,0:T(8,128)}, f32[2,2,2,48,768]{4,3,2,1,0:T(8,128)}, u32[]{:S(2)}, u32[]{:S(2)}) collective-permute-start(f32[2,2,2,48,768]{4,3,2,1,0:T(8,128)} %get-tuple-element.314), channel_id=1, source_target_pairs={{0,2},{2,0},{4,6},{6,4},{8,10},{10,8},{12,14},{14,12},{16,18},{18,... | collective-permute-start | bytes 3538952 | tf_op jit(solution)/shard_map/ppermute | solution.py:395
  187.6 24.9 %collective-permute-start.26 = (f32[2,2,48,1152]{3,2,1,0:T(8,128)S(1)}, f32[2,2,48,1152]{3,2,1,0:T(8,128)S(1)}, u32[]{:S(2)}, u32[]{:S(2)}) collective-permute-start(f32[2,2,48,1152]{3,2,1,0:T(8,128)S(1)} %get-tuple-element.433), channel_id=1, source_target_pairs={{0,4},{2,6},{4,0},{6,2},{8,12},{10,14},{12,8},{14,10},{16,20},{18,... | collective-permute-start | bytes 2654216 | tf_op jit(solution)/shard_map/ppermute | solution.py:395
  190.0 22.5 %collective-permute-start.25 = (f32[2,2,48,768]{3,2,1,0:T(8,128)S(1)}, f32[2,2,48,768]{3,2,1,0:T(8,128)S(1)}, u32[]{:S(2)}, u32[]{:S(2)}) collective-permute-start(f32[2,2,48,768]{3,2,1,0:T(8,128)S(1)} %get-tuple-element.439), channel_id=1, source_target_pairs={{0,8},{2,10},{4,12},{6,14},{8,0},{10,2},{12,4},{14,6},{16,24},{18,... | collective-permute-start | bytes 1769480 | tf_op jit(solution)/shard_map/ppermute | solution.py:395
  190.1 22.4 %collective-permute-start.27 = (f32[256,768]{1,0:T(8,128)S(1)}, f32[256,768]{1,0:T(8,128)S(1)}, u32[]{:S(2)}, u32[]{:S(2)}) collective-permute-start(f32[256,768]{1,0:T(8,128)S(1)} %copy-done.2), channel_id=1, source_target_pairs={{0,1},{1,0},{2,3},{3,2},{4,5},{5,4},{6,7},{7,6},{8,9},{9,8},{10,11... | collective-permute-start | bytes 2359304 | tf_op jit(solution)/shard_map/ppermute | solution.py:392
  213.8 18.3 %collective-permute-start.29 = (f32[2,48,1152]{2,1,0:T(8,128)S(1)}, f32[2,48,1152]{2,1,0:T(8,128)}, u32[]{:S(2)}, u32[]{:S(2)}) collective-permute-start(f32[2,48,1152]{2,1,0:T(8,128)S(1)} %get-tuple-element.442), channel_id=1, source_target_pairs={{0,8},{2,10},{4,12},{6,14},{8,0},{10,2},{12,4},{14,6},{16,24},{18,... | collective-permute-start | bytes 1327112 | tf_op jit(solution)/shard_map/ppermute | solution.py:395
  213.8 18.9 %collective-permute-start.30 = (f32[256,768]{1,0:T(8,128)S(1)}, f32[256,768]{1,0:T(8,128)S(1)}, u32[]{:S(2)}, u32[]{:S(2)}) collective-permute-start(f32[256,768]{1,0:T(8,128)S(1)} %copy-done.4), channel_id=1, source_target_pairs={{0,1},{1,0},{2,3},{3,2},{4,5},{5,4},{6,7},{7,6},{8,9},{9,8},{10,11... | collective-permute-start | bytes 2359304 | tf_op jit(solution)/shard_map/ppermute | solution.py:392
  233.7 16.6 %collective-permute-start.33 = (f32[2,2,2,64,768]{4,3,2,1,0:T(8,128)}, f32[2,2,2,64,768]{4,3,2,1,0:T(8,128)S(1)}, u32[]{:S(2)}, u32[]{:S(2)}) collective-permute-start(f32[2,2,2,64,768]{4,3,2,1,0:T(8,128)} %get-tuple-element.372), channel_id=1, source_target_pairs={{0,2},{2,0},{4,6},{6,4},{8,10},{10,8},{12,14},{14,12},{16,18},{18,... | collective-permute-start | bytes 4718600 | tf_op jit(solution)/shard_map/ppermute | solution.py:395
  233.8 16.6 %collective-permute-start.34 = (f32[2,2,2,48,384]{4,3,2,1,0:T(8,128)S(1)}, f32[2,2,2,48,384]{4,3,2,1,0:T(8,128)S(1)}, u32[]{:S(2)}, u32[]{:S(2)}) collective-permute-start(f32[2,2,2,48,384]{4,3,2,1,0:T(8,128)S(1)} %get-tuple-element.374), channel_id=1, source_target_pairs={{0,2},{2,0},{4,6},{6,4},{8,10},{10,8},{12,14},{14,12},{16,18},{18,... | collective-permute-start | bytes 1769480 | tf_op jit(solution)/shard_map/ppermute | solution.py:395
  250.6 18.9 %collective-permute-start.36 = (f32[2,2,64,768]{3,2,1,0:T(8,128)S(1)}, f32[2,2,64,768]{3,2,1,0:T(8,128)S(1)}, u32[]{:S(2)}, u32[]{:S(2)}) collective-permute-start(f32[2,2,64,768]{3,2,1,0:T(8,128)S(1)} %get-tuple-element.436), channel_id=1, source_target_pairs={{0,4},{2,6},{4,0},{6,2},{8,12},{10,14},{12,8},{14,10},{16,20},{18,... | collective-permute-start | bytes 2359304 | tf_op jit(solution)/shard_map/ppermute | solution.py:395
  252.0 18.5 %collective-permute-start.38 = (f32[256,768]{1,0:T(8,128)S(1)}, f32[256,768]{1,0:T(8,128)S(1)}, u32[]{:S(2)}, u32[]{:S(2)}) collective-permute-start(f32[256,768]{1,0:T(8,128)S(1)} %copy-done), channel_id=1, source_target_pairs={{0,1},{1,0},{2,3},{3,2},{4,5},{5,4},{6,7},{7,6},{8,9},{9,8},{10,11... | collective-permute-start | bytes 2359304 | tf_op jit(solution)/shard_map/ppermute | solution.py:392
  (93 other events, 780.1 us)
Sparse Core Ops, SparseCore 0:
  35.5 65.9 all-gather.1
  137.0 80.4 reduce-scatter.1

commit v2 on v1

--- a/solution.py
+++ b/solution.py
@@ -348,13 +348,12 @@
     up, qkv = up_ref[...], ka_ref[...] + kb_ref[...]
     pieces = [f_ref[:3], a_ref[:3]] + [
         up[:1, at * width:(at + 1) * width] for at in range(up.shape[1] // width)
-    ] + [jnp.concatenate([qkv[:1, :half], qkv[:1, 2 * half:]], axis=1)]
-    have = sum(piece.shape[0] for piece in pieces)
-    pieces.append(jnp.zeros((-have % 16, width), F32))
+    ]
     extra = jnp.concatenate(pieces, axis=0)
+    biases = jnp.concatenate([qkv[:1, :half], qkv[:1, 2 * half:], jnp.zeros((6, half), F32)], axis=0)
     turn((x_ref,), turned)
     put(nn(turned[...], dqkv_ref[:, :2 * half]), core_ref, outs[:count], rows, LAST_ORDERS[0], extra)
-    put(nn(turned[...], dqkv_ref[:, 2 * half:]), core_ref, outs[count:], rows, LAST_ORDERS[1])
+    put(nn(turned[...], dqkv_ref[:, 2 * half:]), core_ref, outs[count:], rows, LAST_ORDERS[1], biases)
 
 
 def join_pieces(place_ref, *refs):
@@ -624,30 +623,35 @@
     dqkv, sums_a, mine_a = back_attend(0, d_context, (), (256, 256))
     dqkv, mine_a, d_context = advance(up, dqkv, mine_a, d_context)
     theirs_a = [swap_mp(mine_a[0])]
-    dqkv, sums_b, mine_b = back_attend(1, d_context, (dqkv,), (128, 256, 128))
-    dqkv, mine_a, mine_b, theirs_a = advance(up, dqkv, mine_a, mine_b, theirs_a)
-    theirs_a.append(swap_mp(mine_a[1]))
+    dqkv, sums_b, mine_b = back_attend(1, d_context, (dqkv,), (256, 128, 128))
+    sums_rows = 6 + units // width
     last = call(
         functools.partial(gradient_attention, lead[-1]), (1,),
         [(core_arg, "smem", None), full(inputs), full(dqkv)]
         + [full(a) for a in (stats_ffn, stats_attn, sums_up, sums_a, sums_b)],
-        parted(2 * half, 2 * half, lambda i: 0, 16) + parted(half, half, lambda i: 0),
+        parted(2 * half, 2 * half, lambda i: 0, sums_rows) + parted(half, half, lambda i: 0, 8),
         [turned], 7.0,
     )
-    last, mine_b, theirs_a, down_part = advance(up, last, mine_b, theirs_a, down_part)
+    last, mine_a, mine_b, theirs_a = advance(up, last, mine_a, mine_b, theirs_a)
     query, value = [Reduction(parts, order) for parts, order in zip(pairs(last), LAST_ORDERS)]
+    theirs_a.append(swap_mp(mine_a[1]))
+    mine_b, theirs_a, down_part = advance(up + [query, value], mine_b, theirs_a, down_part)
     theirs_b = []
-    for moving in (up + [query, value], [query, value], [query, value]):
+    for moving in (up + [query, value], [query, value]):
         theirs_b.append(swap_mp(mine_b[len(theirs_b)]))
         mine_b, theirs_b = advance(moving, mine_b, theirs_b)
+    theirs_b.append(swap_mp(mine_b[2]))
     if split:
         query_part, value_part = query.result(), value.result()
-        vectors = query_part[shard:]
+        vectors, biases = query_part[shard:], value_part[shard:]
     else:
-        (whole,) = query.parts
-        vectors = lax.psum(whole[width:], "dp")
-        query_part = lax.psum_scatter(whole[:width], "dp", scatter_dimension=0, tiled=True)
-        value_part = value.result()
+        (whole,), (value_whole,) = query.parts, value.parts
+        vectors, biases = lax.psum((whole[width:], value_whole[width:]), "dp")
+        query_part, value_part = (
+            lax.psum_scatter(one[:width], "dp", scatter_dimension=0, tiled=True)
+            for one in (whole, value_whole)
+        )
+    value_part = value_part[:shard]
     query_part = query_part[:shard]
     up_part = [one.result() for one in up]
     proj_part = up_part[1][:, units // 2:]
@@ -669,8 +673,8 @@
         query_part[:, :half],
         query_part[:, half:],
         value_part,
-        vectors[8, :half],
-        vectors[8, half:],
+        biases[0],
+        biases[1],
         proj_part.T,
         vectors[5],
         vectors[3],

time: 307 us -> 301 us (0.980)
  waiting for transfers between devices: 68.5 us -> 56.2 us
  starting transfers between devices: 49.3 us -> 53.3 us
  other arithmetic: 12 us -> 15.6 us
    ppermute x34, waiting for transfers between devices: 65.2 us -> 53.1 us  [swap_dp(): return lax.ppermute(array, 'dp', [(i, i ^ bit) for i in range(dp)])]
    ppermute x34, starting transfers between devices: 34.3 us -> 41.2 us  [swap_dp(): return lax.ppermute(array, 'dp', [(i, i ^ bit) for i in range(dp)])]
    add x12, other arithmetic: 7.83 us -> 12.1 us  [step(): send = sum((pick(term, 1 - bit, 0) for term in self.terms))]
    unnamed x144 -> x130, local copies, waits for them, and re-layouts: 17.7 us -> 15.6 us
  transfers between devices with their start and end apart: 46 -> 46, of which waited for: 22 -> 18; matrix products, arithmetic and copies ran while one was open for 5% -> 7% of each run, Pallas kernels for 38% -> 38%
where the time goes in v2:
time: 301 us; the launch traced here: 297 us
  Pallas kernels  132 us (44%)
  waiting for transfers between devices  56.2 us (19%)
  starting transfers between devices  53.3 us (18%)
  local copies, waits for them, and re-layouts  23.9 us (8%)
  other arithmetic  15.6 us (5%)
  between operations  15.1 us (5%)
    pallas_call x17, Pallas kernels, call(): pl.pallas_call(body, grid=grid, in_specs=[spec(a.shape, b, i) for a, b, i...  132 us
    ppermute x34, waiting for transfers between devices, swap_dp(): return lax.ppermute(array, 'dp', [(i, i ^ bit) for i in range(dp)])  53.1 us
    ppermute x34, starting transfers between devices, swap_dp(): return lax.ppermute(array, 'dp', [(i, i ^ bit) for i in range(dp)])  41.2 us
    unnamed x130, local copies, waits for them, and re-layouts  15.6 us
    add x12, other arithmetic, step(): send = sum((pick(term, 1 - bit, 0) for term in self.terms))  12.1 us
    ppermute x10, starting transfers between devices, swap_mp(): return lax.ppermute(array, 'mp', [(0, 1), (1, 0)])  11.5 us
  transfers between devices with their start and end apart: 46, of which 18 were waited for; matrix products, arithmetic and copies ran while one was open for 7% of the time, Pallas kernels for 38%

profile of v2, /device:TPU:0, one launch (start us, length us, event | category | flops | bytes accessed | tf_op | source)
XLA Modules:
  0.0 296.7 jit_solution(4501719035613062857)
XLA Ops:
  21.3 10.0 %shard_map.314 = (bf16[512,384]{1,0:T(8,128)(2,1)S(1)}, bf16[512,384]{1,0:T(8,128)(2,1)S(1)}, bf16[512,384]{1,0:T(8,128)(2,1)S(1)}, bf16[512,384]{1,0:T(8,128)(2...) custom-call(bf16[1024,768]{1,0:T(8,128)(2,1)} %x_ref.7, bf16[768,384]{1,0:T(8,128)(2,1)S(1)} %copy-done.10, ...), custom_call_target="tpu_custom_call" | custom-call | flops 10350000128 | bytes 5741568 | tf_op jit(solution)/shard_map/pallas_call | solution.py:45
  45.4 9.9 %shard_map.315 = (bf16[512,384]{1,0:T(8,128)(2,1)S(1)}, bf16[512,384]{1,0:T(8,128)(2,1)S(1)}, bf16[512,384]{1,0:T(8,128)(2,1)S(1)}, bf16[512,384]{1,0:T(8,128)(2...) custom-call(bf16[1024,768]{1,0:T(8,128)(2,1)} %x_ref.7, bf16[768,384]{1,0:T(8,128)(2,1)S(1)} %copy-done.10, ...), custom_call_target="tpu_custom_call" | custom-call | flops 10350000128 | bytes 5729280 | tf_op jit(solution)/shard_map/pallas_call | solution.py:45
  56.1 3.3 %collective-permute-done.6.refs_1_ = f32[96,1536]{1,0:T(8,128)S(1)} collective-permute-done((f32[96,1536]{1,0:T(8,128)}, f32[96,1536]{1,0:T(8,128)S(1)}, u32[]{:S(2)}, u32[]{:S(2)}) %collective-permute-start.6) | collective-permute-done | bytes 589856 | tf_op jit(solution)/shard_map/ppermute | solution.py:394
  59.4 6.6 %collective-permute-done.7.refs_2_ = f32[96,1536]{1,0:T(8,128)S(1)} collective-permute-done((f32[96,1536]{1,0:T(8,128)}, f32[96,1536]{1,0:T(8,128)S(1)}, u32[]{:S(2)}, u32[]{:S(2)}) %collective-permute-start.7) | collective-permute-done | bytes 589856 | tf_op jit(solution)/shard_map/ppermute | solution.py:394
  72.2 8.8 %shard_map.317 = (bf16[512,768]{1,0:T(8,128)(2,1)S(1)}, f32[512,768]{1,0:T(8,128)}, f32[1024,768]{1,0:T(8,128)}, bf16[1024,1536]{1,0:T(8,128)(2,1)}, bf16[1024,1536]{1,0:T(8,128)(2,1)}) custom-call(bf16[1024,768]{1,0:T(8,128)(2,1)} %x_ref.7, bf16[512,384]{1,0:T(8,128)(2,1)S(1)} %copy-done.29, f32[520,384]{1,0:T(8,128)S(1)} %collective-permute-done.5.cx_ref.bu_ref, ...), custom_call_target="tpu_custom_call" | custom-call | flops 9200000000 | bytes 20477952 | tf_op jit(solution)/shard_map/pallas_call | solution.py:45
  82.6 8.6 %collective-permute-done.15.refs_4_ = f32[48,1536]{1,0:T(8,128)S(1)} collective-permute-done((f32[48,1536]{1,0:T(8,128)S(1)}, f32[48,1536]{1,0:T(8,128)S(1)}, u32[]{:S(2)}, u32[]{:S(2)}) %collective-permute-start.15) | collective-permute-done | bytes 294944 | tf_op jit(solution)/shard_map/ppermute | solution.py:394
  98.1 4.6 %shard_map.320 = (bf16[1024,1536]{1,0:T(8,128)(2,1)}, bf16[1024,1536]{1,0:T(8,128)(2,1)}) custom-call(bf16[512,768]{1,0:T(8,128)(2,1)S(1)} %get-tuple-element.282.nlow_ref.la_ref, bf16[768,1536]{1,0:T(8,128)(2,1)S(1)} %copy-done.15, f32[520,384]{1,0:T(8,128)S(1)} %collective-permute-done.5.cx_ref.bu_ref), custom_call_target="tpu_custom_call" | custom-call | flops 4600000000 | bytes 10235904 | tf_op jit(solution)/shard_map/pallas_call | solution.py:45
  102.6 8.6 %shard_map.318 = (bf16[512,768]{1,0:T(8,128)(2,1)S(1)}, f32[512,768]{1,0:T(8,128)}, f32[1024,768]{1,0:T(8,128)}, bf16[1024,1536]{1,0:T(8,128)(2,1)}, bf16[1024,1536]{1,0:T(8,128)(2,1)}) custom-call(bf16[1024,768]{1,0:T(8,128)(2,1)} %x_ref.7, bf16[512,384]{1,0:T(8,128)(2,1)S(1)} %copy-done.25, ...), custom_call_target="tpu_custom_call", output_to_operand_aliasing={{2}: (12, {}), {3}: (13, {}), {4}: (14, {})} | custom-call | flops 9200000000 | bytes 29902848 | tf_op jit(solution)/shard_map/pallas_call | solution.py:45
  111.3 4.7 %shard_map.321 = (bf16[1024,1536]{1,0:T(8,128)(2,1)}, bf16[1024,1536]{1,0:T(8,128)(2,1)}) custom-call(bf16[512,768]{1,0:T(8,128)(2,1)S(1)} %get-tuple-element.271.nlow_ref.lb_ref, bf16[768,1536]{1,0:T(8,128)(2,1)S(1)} %copy-done.16, f32[520,384]{1,0:T(8,128)S(1)} %collective-permute-done.5.cx_ref.bu_ref, ...), custom_call_target="tpu_custom_call", output_to_operand_aliasing={{0}: (3, {}), {1}: (4, {})} | custom-call | flops 4600000000 | bytes 16527360 | tf_op jit(solution)/shard_map/pallas_call | solution.py:45
  118.4 11.5 %shard_map.322 = (bf16[1024,768]{1,0:T(8,128)(2,1)}, f32[1024,768]{1,0:T(8,128)}, bf16[1024,768]{1,0:T(8,128)(2,1)S(1)}, f32[8,768]{1,0:T(8,128)S(1)}, bf16[768,1536]{1,0:T(8,128)(2,1)}) custom-call(bf16[1024,1536]{1,0:T(8,128)(2,1)} %get-tuple-element.285.act_ref, f32[512,768]{1,0:T(8,128)S(1)} %copy-done.22, f32[512,768]{1,0:T(8,128)} %get-tuple-element.287.startb_ref, ...), custom_call_target="tpu_custom_call" | custom-call | flops 11500000256 | bytes 21264384 | tf_op jit(solution)/shard_map/pallas_call | solution.py:45
  129.8 6.7 %shard_map.323 = f32[768,1536]{1,0:T(8,128)} custom-call(bf16[1024,768]{1,0:T(8,128)(2,1)S(1)} %get-tuple-element.292.left_ref.dffn_ref, bf16[1024,1536]{1,0:T(8,128)(2,1)} %get-tuple-element.291.right_ref), custom_call_target="tpu_custom_call" | custom-call | flops 6899999744 | bytes 9437184 | tf_op jit(solution)/shard_map/pallas_call | solution.py:45
  137.8 20.8 %shard_map.324 = (bf16[1024,1536]{1,0:T(8,128)(2,1)}, f32[8,1536]{1,0:T(8,128)S(1)}, f32[1024,768]{1,0:T(8,128)}, bf16[1024,768]{1,0:T(8,128)(2,1)S(1)}, bf16[10...) custom-call(bf16[1024,768]{1,0:T(8,128)(2,1)} %copy-done.19, bf16[1024,1536]{1,0:T(8,128)(2,1)} %get-tuple-element.293.so_ref, ...), custom_call_target="tpu_custom_call" | custom-call | flops 23000000512 | bytes 32910336 | tf_op jit(solution)/shard_map/pallas_call | solution.py:45
  160.6 9.7 %shard_map.325 = (f32[2,2,2,48,768]{4,3,2,1,0:T(8,128)S(1)}, f32[2,2,2,48,768]{4,3,2,1,0:T(8,128)}, f32[2,2,2,48,1152]{4,3,2,1,0:T(8,128)}, f32[2,2,2,48,1152]{4,3,2,1,0:T(8,128)}) custom-call(s32[1]{0:T(128)} %bitcast.8.core_ref, bf16[512,768]{1,0:T(8,128)(2,1)S(1)} %copy-done.21, bf16[512,768]{1,0:T(8,128)(2,1)S(1)} %copy-done.18, ...), custom_call_target="tpu_custom_call" | custom-call | flops 10350000128 | bytes 12976132 | tf_op jit(solution)/shard_map/pallas_call | solution.py:45
  174.9 10.7 %shard_map.326 = (bf16[1024,1152]{1,0:T(8,128)(2,1)}, f32[8,1152]{1,0:T(8,128)S(1)}, f32[256,768]{1,0:T(8,128)}, f32[256,768]{1,0:T(8,128)}) custom-call(bf16[512,384]{1,0:T(8,128)(2,1)S(1)} %copy-done.38, bf16[512,384]{1,0:T(8,128)(2,1)S(1)} %copy-done.40, bf16[512,384]{1,0:T(8,128)(2,1)S(1)} %copy-done.42, f32[6,512]{1,0:T(8,128)S(1)} %get-tuple-element.313.lse_ref, ...), custom_call_target="tpu_custom_call" | custom-call | flops 10350000128 | bytes 7723008 | tf_op jit(solution)/shard_map/pallas_call | solution.py:45
  191.6 10.7 %shard_map.327 = (bf16[1024,1152]{1,0:T(8,128)(2,1)}, f32[8,1152]{1,0:T(8,128)S(1)}, f32[256,768]{1,0:T(8,128)}, f32[128,768]{1,0:T(8,128)S(1)}, f32[128,768]{1,0:T(8,128)S(1)}) custom-call(bf16[512,384]{1,0:T(8,128)(2,1)S(1)} %copy-done.32, bf16[512,384]{1,0:T(8,128)(2,1)S(1)} %copy-done.34, ...), custom_call_target="tpu_custom_call", output_to_operand_aliasing={{0}: (11, {})} | custom-call | flops 10350000128 | bytes 10082304 | tf_op jit(solution)/shard_map/pallas_call | solution.py:45
  202.4 5.8 %shard_map.328 = (f32[2,2,2,56,768]{4,3,2,1,0:T(8,128)S(1)}, f32[2,2,2,56,768]{4,3,2,1,0:T(8,128)}, f32[2,2,2,56,384]{4,3,2,1,0:T(8,128)S(1)}, f32[2,2,2,56,384]{4,3,2,1,0:T(8,128)}) custom-call(s32[1]{0:T(128)} %bitcast.8.core_ref, bf16[1024,768]{1,0:T(8,128)(2,1)} %x_ref.7, bf16[1024,1152]{1,0:T(8,128)(2,1)} %get-tuple-element.328.dqkv_ref, ...), custom_call_target="tpu_custom_call" | custom-call | flops 8049999872 | bytes 8232964 | tf_op jit(solution)/shard_map/pallas_call | solution.py:45
  208.2 4.5 %collective-permute-done.25 = f32[2,2,48,768]{3,2,1,0:T(8,128)} collective-permute-done((f32[2,2,48,768]{3,2,1,0:T(8,128)S(1)}, f32[2,2,48,768]{3,2,1,0:T(8,128)}, u32[]{:S(2)}, u32[]{:S(2)}) %collective-permute-start.25) | collective-permute-done | bytes 589856 | tf_op jit(solution)/shard_map/ppermute | solution.py:394
  218.8 6.0 %collective-permute-start.28 = (f32[2,48,768]{2,1,0:T(8,128)S(1)}, f32[2,48,768]{2,1,0:T(8,128)S(1)}, u32[]{:S(2)}, u32[]{:S(2)}) collective-permute-start(f32[2,48,768]{2,1,0:T(8,128)S(1)} %get-tuple-element.439), channel_id=1, source_target_pairs={{0,16},{2,18},{4,20},{6,22},{8,24},{10,26},{12,28},{14,30},{16,0},... | collective-permute-start | bytes 884744 | tf_op jit(solution)/shard_map/ppermute | solution.py:394
  224.9 8.4 %collective-permute-done.28 = f32[2,48,768]{2,1,0:T(8,128)S(1)} collective-permute-done((f32[2,48,768]{2,1,0:T(8,128)S(1)}, f32[2,48,768]{2,1,0:T(8,128)S(1)}, u32[]{:S(2)}, u32[]{:S(2)}) %collective-permute-start.28) | collective-permute-done | bytes 294944 | tf_op jit(solution)/shard_map/ppermute | solution.py:394
  239.8 5.9 %collective-permute-start.36 = (f32[2,2,56,384]{3,2,1,0:T(8,128)S(1)}, f32[2,2,56,384]{3,2,1,0:T(8,128)S(1)}, u32[]{:S(2)}, u32[]{:S(2)}) collective-permute-start(f32[2,2,56,384]{3,2,1,0:T(8,128)S(1)} %get-tuple-element.436), channel_id=1, source_target_pairs={{0,8},{2,10},{4,12},{6,14},{8,0},{10,2},{12,4},{14,6},{16,24},{18,... | collective-permute-start | bytes 1032200 | tf_op jit(solution)/shard_map/ppermute | solution.py:394
  252.9 4.4 %collective-permute-done.33 = f32[48,768]{1,0:T(8,128)S(1)} collective-permute-done((f32[48,768]{1,0:T(8,128)S(1)}, f32[48,768]{1,0:T(8,128)S(1)}, u32[]{:S(2)}, u32[]{:S(2)}) %collective-permute-start.33) | collective-permute-done | bytes 147488 | tf_op jit(solution)/shard_map/ppermute | solution.py:394
  260.9 3.7 %collective-permute-start.38 = (f32[2,56,768]{2,1,0:T(8,128)S(1)}, f32[2,56,768]{2,1,0:T(8,128)S(1)}, u32[]{:S(2)}, u32[]{:S(2)}) collective-permute-start(f32[2,56,768]{2,1,0:T(8,128)S(1)} %get-tuple-element.432), channel_id=1, source_target_pairs={{0,8},{2,10},{4,12},{6,14},{8,0},{10,2},{12,4},{14,6},{16,24},{18,... | collective-permute-start | bytes 1032200 | tf_op jit(solution)/shard_map/ppermute | solution.py:394
  267.6 5.1 %collective-permute-done.38 = f32[2,56,768]{2,1,0:T(8,128)S(1)} collective-permute-done((f32[2,56,768]{2,1,0:T(8,128)S(1)}, f32[2,56,768]{2,1,0:T(8,128)S(1)}, u32[]{:S(2)}, u32[]{:S(2)}) %collective-permute-start.38) | collective-permute-done | bytes 344096 | tf_op jit(solution)/shard_map/ppermute | solution.py:394
  279.9 4.3 %collective-permute-done.42 = f32[56,768]{1,0:T(8,128)S(1)} collective-permute-done((f32[56,768]{1,0:T(8,128)S(1)}, f32[56,768]{1,0:T(8,128)S(1)}, u32[]{:S(2)}, u32[]{:S(2)}) %collective-permute-start.42) | collective-permute-done | bytes 172064 | tf_op jit(solution)/shard_map/ppermute | solution.py:394
  (267 shorter events, 98.1 us)
Async XLA Ops:
  7.3 109.7 %all-gather.2.cloned.1.call-start = ((), (), s32[]{:S(2)}) async-start(), calls=%async_computation.1 | async-start | bytes 5013504 | tf_op jit(solution)/shard_map/all_gather | solution.py:459
  13.9 19.6 %collective-permute-start.4 = (f32[48,1536]{1,0:T(8,128)}, f32[48,1536]{1,0:T(8,128)}, u32[]{:S(2)}, u32[]{:S(2)}) collective-permute-start(f32[48,1536]{1,0:T(8,128)} %convert_bitcast_fusion), channel_id=1, source_target_pairs={{0,1},{1,0},{2,3},{3,2},{4,5},{5,4},{6,7},{7,6},{8,9},{9,8},{10,11... | collective-permute-start | bytes 884744 | tf_op jit(solution)/shard_map/ppermute | solution.py:391
  16.2 17.3 %collective-permute-start.1 = (f32[96,384]{1,0:T(8,128)S(1)}, f32[96,384]{1,0:T(8,128)S(1)}, u32[]{:S(2)}, u32[]{:S(2)}) collective-permute-start(f32[96,384]{1,0:T(8,128)S(1)} %collective-permute-done.refs_0_), channel_id=1, source_target_pairs={{0,4},{2,6},{4,0},{6,2},{8,12},{10,14},{12,8},{14,10},{16,20},{18,... | collective-permute-start | bytes 442376 | tf_op jit(solution)/shard_map/ppermute | solution.py:394
  18.1 15.4 %collective-permute-start.2 = (f32[96,384]{1,0:T(8,128)S(1)}, f32[96,384]{1,0:T(8,128)S(1)}, u32[]{:S(2)}, u32[]{:S(2)}) collective-permute-start(f32[96,384]{1,0:T(8,128)S(1)} %collective-permute-done.refs_0_), channel_id=1, source_target_pairs={{0,8},{2,10},{4,12},{6,14},{8,0},{10,2},{12,4},{14,6},{16,24},{18,... | collective-permute-start | bytes 442376 | tf_op jit(solution)/shard_map/ppermute | solution.py:394
  19.7 15.6 %collective-permute-start.3 = (f32[96,1536]{1,0:T(8,128)}, f32[96,1536]{1,0:T(8,128)}, u32[]{:S(2)}, u32[]{:S(2)}) collective-permute-start(f32[96,1536]{1,0:T(8,128)} %dynamic-slice_convert_fusion), channel_id=1, source_target_pairs={{0,1},{1,0},{2,3},{3,2},{4,5},{5,4},{6,7},{7,6},{8,9},{9,8},{10,11... | collective-permute-start | bytes 1769480 | tf_op jit(solution)/shard_map/ppermute | solution.py:391
  35.3 200.2 %reduce-scatter.2.cloned.1.call-start = ((), (), s32[]{:S(2)}) async-start(), calls=%async_computation.2 | async-start | bytes 5013504 | tf_op jit(solution)/shard_map/reduce_scatter | solution.py:575
  41.2 18.2 %collective-permute-start.6 = (f32[96,1536]{1,0:T(8,128)}, f32[96,1536]{1,0:T(8,128)S(1)}, u32[]{:S(2)}, u32[]{:S(2)}) collective-permute-start(f32[96,1536]{1,0:T(8,128)} %collective-permute-done.3.refs_0_), channel_id=1, source_target_pairs={{0,4},{2,6},{4,0},{6,2},{8,12},{10,14},{12,8},{14,10},{16,20},{18,... | collective-permute-start | bytes 1769480 | tf_op jit(solution)/shard_map/ppermute | solution.py:394
  41.8 24.2 %collective-permute-start.7 = (f32[96,1536]{1,0:T(8,128)}, f32[96,1536]{1,0:T(8,128)S(1)}, u32[]{:S(2)}, u32[]{:S(2)}) collective-permute-start(f32[96,1536]{1,0:T(8,128)} %collective-permute-done.3.refs_0_), channel_id=1, source_target_pairs={{0,8},{2,10},{4,12},{6,14},{8,0},{10,2},{12,4},{14,6},{16,24},{18,... | collective-permute-start | bytes 1769480 | tf_op jit(solution)/shard_map/ppermute | solution.py:394
  43.8 27.2 %collective-permute-start.16 = (f32[96,1536]{1,0:T(8,128)}, f32[96,1536]{1,0:T(8,128)S(1)}, u32[]{:S(2)}, u32[]{:S(2)}) collective-permute-start(f32[96,1536]{1,0:T(8,128)} %collective-permute-done.3.refs_0_), channel_id=1, source_target_pairs={{0,2},{2,0},{4,6},{6,4},{8,10},{10,8},{12,14},{14,12},{16,18},{18,... | collective-permute-start | bytes 1769480 | tf_op jit(solution)/shard_map/ppermute | solution.py:394
  44.3 21.7 %collective-permute-start.5 = (f32[520,384]{1,0:T(8,128)}, f32[520,384]{1,0:T(8,128)S(1)}, u32[]{:S(2)}, u32[]{:S(2)}) collective-permute-start(f32[520,384]{1,0:T(8,128)} %get-tuple-element.222), channel_id=1, source_target_pairs={{0,1},{1,0},{2,3},{3,2},{4,5},{5,4},{6,7},{7,6},{8,9},{9,8},{10,11... | collective-permute-start | bytes 2396168 | tf_op jit(solution)/shard_map/ppermute | solution.py:391
  66.6 24.6 %collective-permute-start.17 = (f32[96,1536]{1,0:T(8,128)S(1)}, f32[96,1536]{1,0:T(8,128)S(1)}, u32[]{:S(2)}, u32[]{:S(2)}) collective-permute-start(f32[96,1536]{1,0:T(8,128)S(1)} %collective-permute-done.6.refs_1_), channel_id=1, source_target_pairs={{0,2},{2,0},{4,6},{6,4},{8,10},{10,8},{12,14},{14,12},{16,18},{18,... | collective-permute-start | bytes 1769480 | tf_op jit(solution)/shard_map/ppermute | solution.py:394
  66.7 24.5 %collective-permute-start.18 = (f32[96,1536]{1,0:T(8,128)S(1)}, f32[96,1536]{1,0:T(8,128)S(1)}, u32[]{:S(2)}, u32[]{:S(2)}) collective-permute-start(f32[96,1536]{1,0:T(8,128)S(1)} %collective-permute-done.7.refs_2_), channel_id=1, source_target_pairs={{0,2},{2,0},{4,6},{6,4},{8,10},{10,8},{12,14},{14,12},{16,18},{18,... | collective-permute-start | bytes 1769480 | tf_op jit(solution)/shard_map/ppermute | solution.py:394
  67.3 23.9 %collective-permute-start.13 = (f32[512,384]{1,0:T(8,128)}, f32[512,384]{1,0:T(8,128)S(1)}, u32[]{:S(2)}, u32[]{:S(2)}) collective-permute-start(f32[512,384]{1,0:T(8,128)} %get-tuple-element.237), channel_id=1, source_target_pairs={{0,1},{1,0},{2,3},{3,2},{4,5},{5,4},{6,7},{7,6},{8,9},{9,8},{10,11... | collective-permute-start | bytes 2359304 | tf_op jit(solution)/shard_map/ppermute | solution.py:391
  71.0 20.2 %collective-permute-start.15 = (f32[48,1536]{1,0:T(8,128)S(1)}, f32[48,1536]{1,0:T(8,128)S(1)}, u32[]{:S(2)}, u32[]{:S(2)}) collective-permute-start(f32[48,1536]{1,0:T(8,128)S(1)} %slice.87), channel_id=1, source_target_pairs={{0,8},{2,10},{4,12},{6,14},{8,0},{10,2},{12,4},{14,6},{16,24},{18,... | collective-permute-start | bytes 884744 | tf_op jit(solution)/shard_map/ppermute | solution.py:394
  187.4 26.2 %collective-permute-start.26 = (f32[2,2,48,1152]{3,2,1,0:T(8,128)S(1)}, f32[2,2,48,1152]{3,2,1,0:T(8,128)S(1)}, u32[]{:S(2)}, u32[]{:S(2)}) collective-permute-start(f32[2,2,48,1152]{3,2,1,0:T(8,128)S(1)} %get-tuple-element.419), channel_id=1, source_target_pairs={{0,4},{2,6},{4,0},{6,2},{8,12},{10,14},{12,8},{14,10},{16,20},{18,... | collective-permute-start | bytes 2654216 | tf_op jit(solution)/shard_map/ppermute | solution.py:394
  190.5 22.2 %collective-permute-start.25 = (f32[2,2,48,768]{3,2,1,0:T(8,128)S(1)}, f32[2,2,48,768]{3,2,1,0:T(8,128)}, u32[]{:S(2)}, u32[]{:S(2)}) collective-permute-start(f32[2,2,48,768]{3,2,1,0:T(8,128)S(1)} %get-tuple-element.425), channel_id=1, source_target_pairs={{0,8},{2,10},{4,12},{6,14},{8,0},{10,2},{12,4},{14,6},{16,24},{18,... | collective-permute-start | bytes 1769480 | tf_op jit(solution)/shard_map/ppermute | solution.py:394
  190.5 22.2 %collective-permute-start.27 = (f32[256,768]{1,0:T(8,128)S(1)}, f32[256,768]{1,0:T(8,128)S(1)}, u32[]{:S(2)}, u32[]{:S(2)}) collective-permute-start(f32[256,768]{1,0:T(8,128)S(1)} %copy-done.4), channel_id=1, source_target_pairs={{0,1},{1,0},{2,3},{3,2},{4,5},{5,4},{6,7},{7,6},{8,9},{9,8},{10,11... | collective-permute-start | bytes 2359304 | tf_op jit(solution)/shard_map/ppermute | solution.py:391
  213.6 21.9 %collective-permute-start.30 = (f32[2,2,2,56,768]{4,3,2,1,0:T(8,128)}, f32[2,2,2,56,768]{4,3,2,1,0:T(8,128)}, u32[]{:S(2)}, u32[]{:S(2)}) collective-permute-start(f32[2,2,2,56,768]{4,3,2,1,0:T(8,128)} %get-tuple-element.350), channel_id=1, source_target_pairs={{0,2},{2,0},{4,6},{6,4},{8,10},{10,8},{12,14},{14,12},{16,18},{18,... | collective-permute-start | bytes 4128776 | tf_op jit(solution)/shard_map/ppermute | solution.py:394
  213.6 21.9 %collective-permute-start.32 = (f32[256,768]{1,0:T(8,128)S(1)}, f32[256,768]{1,0:T(8,128)}, u32[]{:S(2)}, u32[]{:S(2)}) collective-permute-start(f32[256,768]{1,0:T(8,128)S(1)} %copy-done.6), channel_id=1, source_target_pairs={{0,1},{1,0},{2,3},{3,2},{4,5},{5,4},{6,7},{7,6},{8,9},{9,8},{10,11... | collective-permute-start | bytes 2359304 | tf_op jit(solution)/shard_map/ppermute | solution.py:391
  215.1 20.5 %collective-permute-start.31 = (f32[2,2,2,56,384]{4,3,2,1,0:T(8,128)}, f32[2,2,2,56,384]{4,3,2,1,0:T(8,128)}, u32[]{:S(2)}, u32[]{:S(2)}) collective-permute-start(f32[2,2,2,56,384]{4,3,2,1,0:T(8,128)} %get-tuple-element.352), channel_id=1, source_target_pairs={{0,2},{2,0},{4,6},{6,4},{8,10},{10,8},{12,14},{14,12},{16,18},{18,... | collective-permute-start | bytes 2064392 | tf_op jit(solution)/shard_map/ppermute | solution.py:394
  216.5 19.1 %collective-permute-start.29 = (f32[2,48,1152]{2,1,0:T(8,128)}, f32[2,48,1152]{2,1,0:T(8,128)}, u32[]{:S(2)}, u32[]{:S(2)}) collective-permute-start(f32[2,48,1152]{2,1,0:T(8,128)} %get-tuple-element.428), channel_id=1, source_target_pairs={{0,8},{2,10},{4,12},{6,14},{8,0},{10,2},{12,4},{14,6},{16,24},{18,... | collective-permute-start | bytes 1327112 | tf_op jit(solution)/shard_map/ppermute | solution.py:394
  237.2 21.6 %collective-permute-start.35 = (f32[2,2,56,768]{3,2,1,0:T(8,128)S(1)}, f32[2,2,56,768]{3,2,1,0:T(8,128)S(1)}, u32[]{:S(2)}, u32[]{:S(2)}) collective-permute-start(f32[2,2,56,768]{3,2,1,0:T(8,128)S(1)} %get-tuple-element.422), channel_id=1, source_target_pairs={{0,4},{2,6},{4,0},{6,2},{8,12},{10,14},{12,8},{14,10},{16,20},{18,... | collective-permute-start | bytes 2064392 | tf_op jit(solution)/shard_map/ppermute | solution.py:394
  238.0 20.8 %collective-permute-start.37 = (f32[256,768]{1,0:T(8,128)S(1)}, f32[256,768]{1,0:T(8,128)S(1)}, u32[]{:S(2)}, u32[]{:S(2)}) collective-permute-start(f32[256,768]{1,0:T(8,128)S(1)} %copy-done), channel_id=1, source_target_pairs={{0,1},{1,0},{2,3},{3,2},{4,5},{5,4},{6,7},{7,6},{8,9},{9,8},{10,11... | collective-permute-start | bytes 2359304 | tf_op jit(solution)/shard_map/ppermute | solution.py:391
  239.8 19.1 %collective-permute-start.36 = (f32[2,2,56,384]{3,2,1,0:T(8,128)S(1)}, f32[2,2,56,384]{3,2,1,0:T(8,128)S(1)}, u32[]{:S(2)}, u32[]{:S(2)}) collective-permute-start(f32[2,2,56,384]{3,2,1,0:T(8,128)S(1)} %get-tuple-element.436), channel_id=1, source_target_pairs={{0,8},{2,10},{4,12},{6,14},{8,0},{10,2},{12,4},{14,6},{16,24},{18,... | collective-permute-start | bytes 1032200 | tf_op jit(solution)/shard_map/ppermute | solution.py:394
  (86 other events, 737.0 us)
Sparse Core Ops, SparseCore 0:
  35.5 65.7 all-gather.1
  137.9 80.1 reduce-scatter.1

commit v3 on v2

--- a/solution.py
+++ b/solution.py
@@ -454,7 +454,7 @@
     down_y = swap_mp(lax.dynamic_slice_in_dim(w_down, d * shard, shard, 1).T.astype(F32))
     saved = [attend(0, lock(inputs, proj)[0])]
     proj, proj_near, up, down_y, saved[0] = lock(
-        proj, near_pieces(proj), swap_mp(lock(eighth(w_up), proj)[0]), down_y, tuple(saved[0])
+        proj, near_pieces(proj), swap_mp(eighth(w_up)), down_y, tuple(saved[0])
     )
     down_oth = lax.all_gather(down_y, "dp", axis=0, tiled=True)
     saved.append(attend(1, lock(inputs, proj)[0]))

time: 301 us -> 301 us (level)
  no operation moved by 1% of the time
where the time goes in v3:
time: 301 us; the launch traced here: 297 us
  Pallas kernels  133 us (44%)
  waiting for transfers between devices  56.2 us (19%)
  starting transfers between devices  53.4 us (18%)
  local copies, waits for them, and re-layouts  23.8 us (8%)
  other arithmetic  15.7 us (5%)
  between operations  15.2 us (5%)
    pallas_call x17, Pallas kernels, call(): pl.pallas_call(body, grid=grid, in_specs=[spec(a.shape, b, i) for a, b, i...  133 us
    ppermute x34, waiting for transfers between devices, swap_dp(): return lax.ppermute(array, 'dp', [(i, i ^ bit) for i in range(dp)])  53 us
    ppermute x34, starting transfers between devices, swap_dp(): return lax.ppermute(array, 'dp', [(i, i ^ bit) for i in range(dp)])  41.3 us
    unnamed x130, local copies, waits for them, and re-layouts  15.6 us
    add x12, other arithmetic, step(): send = sum((pick(term, 1 - bit, 0) for term in self.terms))  12.1 us
    ppermute x10, starting transfers between devices, swap_mp(): return lax.ppermute(array, 'mp', [(0, 1), (1, 0)])  11.5 us
  transfers between devices with their start and end apart: 46, of which 18 were waited for; matrix products, arithmetic and copies ran while one was open for 7% of the time, Pallas kernels for 38%

profile of v3, /device:TPU:0, one launch (start us, length us, event | category | flops | bytes accessed | tf_op | source)
XLA Modules:
  0.0 296.9 jit_solution(14269600954683056563)
XLA Ops:
  21.3 10.0 %shard_map.314 = (bf16[512,384]{1,0:T(8,128)(2,1)S(1)}, bf16[512,384]{1,0:T(8,128)(2,1)S(1)}, bf16[512,384]{1,0:T(8,128)(2,1)S(1)}, bf16[512,384]{1,0:T(8,128)(2...) custom-call(bf16[1024,768]{1,0:T(8,128)(2,1)} %x_ref.7, bf16[768,384]{1,0:T(8,128)(2,1)S(1)} %copy-done.10, ...), custom_call_target="tpu_custom_call" | custom-call | flops 10350000128 | bytes 5741568 | tf_op jit(solution)/shard_map/pallas_call | solution.py:45
  45.4 9.9 %shard_map.315 = (bf16[512,384]{1,0:T(8,128)(2,1)S(1)}, bf16[512,384]{1,0:T(8,128)(2,1)S(1)}, bf16[512,384]{1,0:T(8,128)(2,1)S(1)}, bf16[512,384]{1,0:T(8,128)(2...) custom-call(bf16[1024,768]{1,0:T(8,128)(2,1)} %x_ref.7, bf16[768,384]{1,0:T(8,128)(2,1)S(1)} %copy-done.10, ...), custom_call_target="tpu_custom_call" | custom-call | flops 10350000128 | bytes 5729280 | tf_op jit(solution)/shard_map/pallas_call | solution.py:45
  59.0 6.6 %collective-permute-done.7.refs_2_ = f32[96,1536]{1,0:T(8,128)S(1)} collective-permute-done((f32[96,1536]{1,0:T(8,128)}, f32[96,1536]{1,0:T(8,128)S(1)}, u32[]{:S(2)}, u32[]{:S(2)}) %collective-permute-start.7) | collective-permute-done | bytes 589856 | tf_op jit(solution)/shard_map/ppermute | solution.py:394
  72.2 8.8 %shard_map.317 = (bf16[512,768]{1,0:T(8,128)(2,1)S(1)}, f32[512,768]{1,0:T(8,128)}, f32[1024,768]{1,0:T(8,128)}, bf16[1024,1536]{1,0:T(8,128)(2,1)}, bf16[1024,1536]{1,0:T(8,128)(2,1)}) custom-call(bf16[1024,768]{1,0:T(8,128)(2,1)} %x_ref.7, bf16[512,384]{1,0:T(8,128)(2,1)S(1)} %copy-done.29, f32[520,384]{1,0:T(8,128)S(1)} %collective-permute-done.5.cx_ref.bu_ref, ...), custom_call_target="tpu_custom_call" | custom-call | flops 9200000000 | bytes 20477952 | tf_op jit(solution)/shard_map/pallas_call | solution.py:45
  82.6 8.6 %collective-permute-done.15.refs_4_ = f32[48,1536]{1,0:T(8,128)S(1)} collective-permute-done((f32[48,1536]{1,0:T(8,128)S(1)}, f32[48,1536]{1,0:T(8,128)S(1)}, u32[]{:S(2)}, u32[]{:S(2)}) %collective-permute-start.15) | collective-permute-done | bytes 294944 | tf_op jit(solution)/shard_map/ppermute | solution.py:394
  93.3 3.1 %shard_map.319.wu_ref.wux_ref = bf16[768,1536]{1,0:T(8,128)(2,1)} custom-call(s32[2]{0:T(128)S(1)} %pad_add_fusion.place_ref, f32[96,1536]{1,0:T(8,128)} %collective-permute-done.3.refs_0_, f32[96,1536]{1,0:T(8,128)S(1)} %collective-permute-done.6.refs_1_, f32[96,1536]{1,0:T(8,128)S(1)} %collective-permute-done.7.refs_2_, ...), custom_call_target="tpu_custom_call" | custom-call | flops 3449999872 | bytes 7077896 | tf_op jit(solution)/shard_map/pallas_call | solution.py:45
  98.1 4.6 %shard_map.320 = (bf16[1024,1536]{1,0:T(8,128)(2,1)}, bf16[1024,1536]{1,0:T(8,128)(2,1)}) custom-call(bf16[512,768]{1,0:T(8,128)(2,1)S(1)} %get-tuple-element.280.nlow_ref.la_ref, bf16[768,1536]{1,0:T(8,128)(2,1)S(1)} %copy-done.15, f32[520,384]{1,0:T(8,128)S(1)} %collective-permute-done.5.cx_ref.bu_ref), custom_call_target="tpu_custom_call" | custom-call | flops 4600000000 | bytes 10235904 | tf_op jit(solution)/shard_map/pallas_call | solution.py:45
  102.6 8.6 %shard_map.318 = (bf16[512,768]{1,0:T(8,128)(2,1)S(1)}, f32[512,768]{1,0:T(8,128)}, f32[1024,768]{1,0:T(8,128)}, bf16[1024,1536]{1,0:T(8,128)(2,1)}, bf16[1024,1536]{1,0:T(8,128)(2,1)}) custom-call(bf16[1024,768]{1,0:T(8,128)(2,1)} %x_ref.7, bf16[512,384]{1,0:T(8,128)(2,1)S(1)} %copy-done.25, ...), custom_call_target="tpu_custom_call", output_to_operand_aliasing={{2}: (12, {}), {3}: (13, {}), {4}: (14, {})} | custom-call | flops 9200000000 | bytes 29902848 | tf_op jit(solution)/shard_map/pallas_call | solution.py:45
  111.3 4.7 %shard_map.321 = (bf16[1024,1536]{1,0:T(8,128)(2,1)}, bf16[1024,1536]{1,0:T(8,128)(2,1)}) custom-call(bf16[512,768]{1,0:T(8,128)(2,1)S(1)} %get-tuple-element.269.nlow_ref.lb_ref, bf16[768,1536]{1,0:T(8,128)(2,1)S(1)} %copy-done.16, f32[520,384]{1,0:T(8,128)S(1)} %collective-permute-done.5.cx_ref.bu_ref, ...), custom_call_target="tpu_custom_call", output_to_operand_aliasing={{0}: (3, {}), {1}: (4, {})} | custom-call | flops 4600000000 | bytes 16527360 | tf_op jit(solution)/shard_map/pallas_call | solution.py:45
  118.4 11.5 %shard_map.322 = (bf16[1024,768]{1,0:T(8,128)(2,1)}, f32[1024,768]{1,0:T(8,128)}, bf16[1024,768]{1,0:T(8,128)(2,1)S(1)}, f32[8,768]{1,0:T(8,128)S(1)}, bf16[768,1536]{1,0:T(8,128)(2,1)}) custom-call(bf16[1024,1536]{1,0:T(8,128)(2,1)} %get-tuple-element.283.act_ref, f32[512,768]{1,0:T(8,128)S(1)} %copy-done.22, f32[512,768]{1,0:T(8,128)} %get-tuple-element.285.startb_ref, ...), custom_call_target="tpu_custom_call" | custom-call | flops 11500000256 | bytes 21264384 | tf_op jit(solution)/shard_map/pallas_call | solution.py:45
  129.8 6.7 %shard_map.323 = f32[768,1536]{1,0:T(8,128)} custom-call(bf16[1024,768]{1,0:T(8,128)(2,1)S(1)} %get-tuple-element.290.left_ref.dffn_ref, bf16[1024,1536]{1,0:T(8,128)(2,1)} %get-tuple-element.289.right_ref), custom_call_target="tpu_custom_call" | custom-call | flops 6899999744 | bytes 9437184 | tf_op jit(solution)/shard_map/pallas_call | solution.py:45
  137.8 20.8 %shard_map.324 = (bf16[1024,1536]{1,0:T(8,128)(2,1)}, f32[8,1536]{1,0:T(8,128)S(1)}, f32[1024,768]{1,0:T(8,128)}, bf16[1024,768]{1,0:T(8,128)(2,1)S(1)}, bf16[10...) custom-call(bf16[1024,768]{1,0:T(8,128)(2,1)} %copy-done.19, bf16[1024,1536]{1,0:T(8,128)(2,1)} %get-tuple-element.291.so_ref, ...), custom_call_target="tpu_custom_call" | custom-call | flops 23000000512 | bytes 32910336 | tf_op jit(solution)/shard_map/pallas_call | solution.py:45
  160.6 9.7 %shard_map.325 = (f32[2,2,2,48,768]{4,3,2,1,0:T(8,128)S(1)}, f32[2,2,2,48,768]{4,3,2,1,0:T(8,128)}, f32[2,2,2,48,1152]{4,3,2,1,0:T(8,128)}, f32[2,2,2,48,1152]{4,3,2,1,0:T(8,128)}) custom-call(s32[1]{0:T(128)} %bitcast.8.core_ref, bf16[512,768]{1,0:T(8,128)(2,1)S(1)} %copy-done.21, bf16[512,768]{1,0:T(8,128)(2,1)S(1)} %copy-done.18, ...), custom_call_target="tpu_custom_call" | custom-call | flops 10350000128 | bytes 12976132 | tf_op jit(solution)/shard_map/pallas_call | solution.py:45
  174.9 10.7 %shard_map.326 = (bf16[1024,1152]{1,0:T(8,128)(2,1)}, f32[8,1152]{1,0:T(8,128)S(1)}, f32[256,768]{1,0:T(8,128)}, f32[256,768]{1,0:T(8,128)}) custom-call(bf16[512,384]{1,0:T(8,128)(2,1)S(1)} %copy-done.38, bf16[512,384]{1,0:T(8,128)(2,1)S(1)} %copy-done.40, bf16[512,384]{1,0:T(8,128)(2,1)S(1)} %copy-done.42, f32[6,512]{1,0:T(8,128)S(1)} %get-tuple-element.311.lse_ref, ...), custom_call_target="tpu_custom_call" | custom-call | flops 10350000128 | bytes 7723008 | tf_op jit(solution)/shard_map/pallas_call | solution.py:45
  191.3 10.7 %shard_map.327 = (bf16[1024,1152]{1,0:T(8,128)(2,1)}, f32[8,1152]{1,0:T(8,128)S(1)}, f32[256,768]{1,0:T(8,128)}, f32[128,768]{1,0:T(8,128)S(1)}, f32[128,768]{1,0:T(8,128)S(1)}) custom-call(bf16[512,384]{1,0:T(8,128)(2,1)S(1)} %copy-done.32, bf16[512,384]{1,0:T(8,128)(2,1)S(1)} %copy-done.34, ...), custom_call_target="tpu_custom_call", output_to_operand_aliasing={{0}: (11, {})} | custom-call | flops 10350000128 | bytes 10082304 | tf_op jit(solution)/shard_map/pallas_call | solution.py:45
  202.0 5.8 %shard_map.328 = (f32[2,2,2,56,768]{4,3,2,1,0:T(8,128)S(1)}, f32[2,2,2,56,768]{4,3,2,1,0:T(8,128)}, f32[2,2,2,56,384]{4,3,2,1,0:T(8,128)S(1)}, f32[2,2,2,56,384]{4,3,2,1,0:T(8,128)}) custom-call(s32[1]{0:T(128)} %bitcast.8.core_ref, bf16[1024,768]{1,0:T(8,128)(2,1)} %x_ref.7, bf16[1024,1152]{1,0:T(8,128)(2,1)} %get-tuple-element.326.dqkv_ref, ...), custom_call_target="tpu_custom_call" | custom-call | flops 8049999872 | bytes 8232964 | tf_op jit(solution)/shard_map/pallas_call | solution.py:45
  207.8 5.3 %collective-permute-done.25 = f32[2,2,48,768]{3,2,1,0:T(8,128)} collective-permute-done((f32[2,2,48,768]{3,2,1,0:T(8,128)S(1)}, f32[2,2,48,768]{3,2,1,0:T(8,128)}, u32[]{:S(2)}, u32[]{:S(2)}) %collective-permute-start.25) | collective-permute-done | bytes 589856 | tf_op jit(solution)/shard_map/ppermute | solution.py:394
  218.7 6.6 %collective-permute-start.28 = (f32[2,48,768]{2,1,0:T(8,128)S(1)}, f32[2,48,768]{2,1,0:T(8,128)S(1)}, u32[]{:S(2)}, u32[]{:S(2)}) collective-permute-start(f32[2,48,768]{2,1,0:T(8,128)S(1)} %get-tuple-element.437), channel_id=1, source_target_pairs={{0,16},{2,18},{4,20},{6,22},{8,24},{10,26},{12,28},{14,30},{16,0},... | collective-permute-start | bytes 884744 | tf_op jit(solution)/shard_map/ppermute | solution.py:394
  225.4 7.8 %collective-permute-done.28 = f32[2,48,768]{2,1,0:T(8,128)S(1)} collective-permute-done((f32[2,48,768]{2,1,0:T(8,128)S(1)}, f32[2,48,768]{2,1,0:T(8,128)S(1)}, u32[]{:S(2)}, u32[]{:S(2)}) %collective-permute-start.28) | collective-permute-done | bytes 294944 | tf_op jit(solution)/shard_map/ppermute | solution.py:394
  239.6 5.9 %collective-permute-start.36 = (f32[2,2,56,384]{3,2,1,0:T(8,128)S(1)}, f32[2,2,56,384]{3,2,1,0:T(8,128)S(1)}, u32[]{:S(2)}, u32[]{:S(2)}) collective-permute-start(f32[2,2,56,384]{3,2,1,0:T(8,128)S(1)} %get-tuple-element.434), channel_id=1, source_target_pairs={{0,8},{2,10},{4,12},{6,14},{8,0},{10,2},{12,4},{14,6},{16,24},{18,... | collective-permute-start | bytes 1032200 | tf_op jit(solution)/shard_map/ppermute | solution.py:394
  253.0 4.3 %collective-permute-done.33 = f32[48,768]{1,0:T(8,128)S(1)} collective-permute-done((f32[48,768]{1,0:T(8,128)S(1)}, f32[48,768]{1,0:T(8,128)S(1)}, u32[]{:S(2)}, u32[]{:S(2)}) %collective-permute-start.33) | collective-permute-done | bytes 147488 | tf_op jit(solution)/shard_map/ppermute | solution.py:394
  260.8 4.1 %collective-permute-start.38 = (f32[2,56,768]{2,1,0:T(8,128)S(1)}, f32[2,56,768]{2,1,0:T(8,128)S(1)}, u32[]{:S(2)}, u32[]{:S(2)}) collective-permute-start(f32[2,56,768]{2,1,0:T(8,128)S(1)} %get-tuple-element.430), channel_id=1, source_target_pairs={{0,8},{2,10},{4,12},{6,14},{8,0},{10,2},{12,4},{14,6},{16,24},{18,... | collective-permute-start | bytes 1032200 | tf_op jit(solution)/shard_map/ppermute | solution.py:394
  267.3 5.4 %collective-permute-done.38 = f32[2,56,768]{2,1,0:T(8,128)S(1)} collective-permute-done((f32[2,56,768]{2,1,0:T(8,128)S(1)}, f32[2,56,768]{2,1,0:T(8,128)S(1)}, u32[]{:S(2)}, u32[]{:S(2)}) %collective-permute-start.38) | collective-permute-done | bytes 344096 | tf_op jit(solution)/shard_map/ppermute | solution.py:394
  279.8 4.5 %collective-permute-done.42 = f32[56,768]{1,0:T(8,128)S(1)} collective-permute-done((f32[56,768]{1,0:T(8,128)S(1)}, f32[56,768]{1,0:T(8,128)S(1)}, u32[]{:S(2)}, u32[]{:S(2)}) %collective-permute-start.42) | collective-permute-done | bytes 172064 | tf_op jit(solution)/shard_map/ppermute | solution.py:394
  (267 shorter events, 96.9 us)
Async XLA Ops:
  7.3 109.7 %all-gather.2.cloned.1.call-start = ((), (), s32[]{:S(2)}) async-start(), calls=%async_computation.1 | async-start | bytes 5013504 | tf_op jit(solution)/shard_map/all_gather | solution.py:459
  13.5 21.4 %collective-permute-start.3 = (f32[96,1536]{1,0:T(8,128)}, f32[96,1536]{1,0:T(8,128)}, u32[]{:S(2)}, u32[]{:S(2)}) collective-permute-start(f32[96,1536]{1,0:T(8,128)} %dynamic-slice_convert_fusion), channel_id=1, source_target_pairs={{0,1},{1,0},{2,3},{3,2},{4,5},{5,4},{6,7},{7,6},{8,9},{9,8},{10,11... | collective-permute-start | bytes 1769480 | tf_op jit(solution)/shard_map/ppermute | solution.py:391
  15.7 19.2 %collective-permute-start.4 = (f32[48,1536]{1,0:T(8,128)}, f32[48,1536]{1,0:T(8,128)}, u32[]{:S(2)}, u32[]{:S(2)}) collective-permute-start(f32[48,1536]{1,0:T(8,128)} %convert_bitcast_fusion), channel_id=1, source_target_pairs={{0,1},{1,0},{2,3},{3,2},{4,5},{5,4},{6,7},{7,6},{8,9},{9,8},{10,11... | collective-permute-start | bytes 884744 | tf_op jit(solution)/shard_map/ppermute | solution.py:391
  18.2 15.4 %collective-permute-start.1 = (f32[96,384]{1,0:T(8,128)S(1)}, f32[96,384]{1,0:T(8,128)S(1)}, u32[]{:S(2)}, u32[]{:S(2)}) collective-permute-start(f32[96,384]{1,0:T(8,128)S(1)} %collective-permute-done.refs_0_), channel_id=1, source_target_pairs={{0,4},{2,6},{4,0},{6,2},{8,12},{10,14},{12,8},{14,10},{16,20},{18,... | collective-permute-start | bytes 442376 | tf_op jit(solution)/shard_map/ppermute | solution.py:394
  35.0 200.5 %reduce-scatter.2.cloned.1.call-start = ((), (), s32[]{:S(2)}) async-start(), calls=%async_computation.2 | async-start | bytes 5013504 | tf_op jit(solution)/shard_map/reduce_scatter | solution.py:575
  40.8 18.2 %collective-permute-start.6 = (f32[96,1536]{1,0:T(8,128)}, f32[96,1536]{1,0:T(8,128)S(1)}, u32[]{:S(2)}, u32[]{:S(2)}) collective-permute-start(f32[96,1536]{1,0:T(8,128)} %collective-permute-done.3.refs_0_), channel_id=1, source_target_pairs={{0,4},{2,6},{4,0},{6,2},{8,12},{10,14},{12,8},{14,10},{16,20},{18,... | collective-permute-start | bytes 1769480 | tf_op jit(solution)/shard_map/ppermute | solution.py:394
  41.5 24.2 %collective-permute-start.7 = (f32[96,1536]{1,0:T(8,128)}, f32[96,1536]{1,0:T(8,128)S(1)}, u32[]{:S(2)}, u32[]{:S(2)}) collective-permute-start(f32[96,1536]{1,0:T(8,128)} %collective-permute-done.3.refs_0_), channel_id=1, source_target_pairs={{0,8},{2,10},{4,12},{6,14},{8,0},{10,2},{12,4},{14,6},{16,24},{18,... | collective-permute-start | bytes 1769480 | tf_op jit(solution)/shard_map/ppermute | solution.py:394
  43.4 27.5 %collective-permute-start.16 = (f32[96,1536]{1,0:T(8,128)}, f32[96,1536]{1,0:T(8,128)S(1)}, u32[]{:S(2)}, u32[]{:S(2)}) collective-permute-start(f32[96,1536]{1,0:T(8,128)} %collective-permute-done.3.refs_0_), channel_id=1, source_target_pairs={{0,2},{2,0},{4,6},{6,4},{8,10},{10,8},{12,14},{14,12},{16,18},{18,... | collective-permute-start | bytes 1769480 | tf_op jit(solution)/shard_map/ppermute | solution.py:394
  44.0 21.7 %collective-permute-start.5 = (f32[520,384]{1,0:T(8,128)}, f32[520,384]{1,0:T(8,128)S(1)}, u32[]{:S(2)}, u32[]{:S(2)}) collective-permute-start(f32[520,384]{1,0:T(8,128)} %get-tuple-element.220), channel_id=1, source_target_pairs={{0,1},{1,0},{2,3},{3,2},{4,5},{5,4},{6,7},{7,6},{8,9},{9,8},{10,11... | collective-permute-start | bytes 2396168 | tf_op jit(solution)/shard_map/ppermute | solution.py:391
  66.2 25.0 %collective-permute-start.17 = (f32[96,1536]{1,0:T(8,128)S(1)}, f32[96,1536]{1,0:T(8,128)S(1)}, u32[]{:S(2)}, u32[]{:S(2)}) collective-permute-start(f32[96,1536]{1,0:T(8,128)S(1)} %collective-permute-done.6.refs_1_), channel_id=1, source_target_pairs={{0,2},{2,0},{4,6},{6,4},{8,10},{10,8},{12,14},{14,12},{16,18},{18,... | collective-permute-start | bytes 1769480 | tf_op jit(solution)/shard_map/ppermute | solution.py:394
  66.4 24.8 %collective-permute-start.18 = (f32[96,1536]{1,0:T(8,128)S(1)}, f32[96,1536]{1,0:T(8,128)S(1)}, u32[]{:S(2)}, u32[]{:S(2)}) collective-permute-start(f32[96,1536]{1,0:T(8,128)S(1)} %collective-permute-done.7.refs_2_), channel_id=1, source_target_pairs={{0,2},{2,0},{4,6},{6,4},{8,10},{10,8},{12,14},{14,12},{16,18},{18,... | collective-permute-start | bytes 1769480 | tf_op jit(solution)/shard_map/ppermute | solution.py:394
  66.9 24.3 %collective-permute-start.13 = (f32[512,384]{1,0:T(8,128)}, f32[512,384]{1,0:T(8,128)S(1)}, u32[]{:S(2)}, u32[]{:S(2)}) collective-permute-start(f32[512,384]{1,0:T(8,128)} %get-tuple-element.235), channel_id=1, source_target_pairs={{0,1},{1,0},{2,3},{3,2},{4,5},{5,4},{6,7},{7,6},{8,9},{9,8},{10,11... | collective-permute-start | bytes 2359304 | tf_op jit(solution)/shard_map/ppermute | solution.py:391
  71.0 20.2 %collective-permute-start.15 = (f32[48,1536]{1,0:T(8,128)S(1)}, f32[48,1536]{1,0:T(8,128)S(1)}, u32[]{:S(2)}, u32[]{:S(2)}) collective-permute-start(f32[48,1536]{1,0:T(8,128)S(1)} %slice.87), channel_id=1, source_target_pairs={{0,8},{2,10},{4,12},{6,14},{8,0},{10,2},{12,4},{14,6},{16,24},{18,... | collective-permute-start | bytes 884744 | tf_op jit(solution)/shard_map/ppermute | solution.py:394
  170.3 15.4 %collective-permute-start.24 = (f32[2,2,2,48,1152]{4,3,2,1,0:T(8,128)}, f32[2,2,2,48,1152]{4,3,2,1,0:T(8,128)}, u32[]{:S(2)}, u32[]{:S(2)}) collective-permute-start(f32[2,2,2,48,1152]{4,3,2,1,0:T(8,128)} %get-tuple-element.307), channel_id=1, source_target_pairs={{0,2},{2,0},{4,6},{6,4},{8,10},{10,8},{12,14},{14,12},{16,18},{18,... | collective-permute-start | bytes 5308424 | tf_op jit(solution)/shard_map/ppermute | solution.py:394
  187.4 26.7 %collective-permute-start.26 = (f32[2,2,48,1152]{3,2,1,0:T(8,128)S(1)}, f32[2,2,48,1152]{3,2,1,0:T(8,128)S(1)}, u32[]{:S(2)}, u32[]{:S(2)}) collective-permute-start(f32[2,2,48,1152]{3,2,1,0:T(8,128)S(1)} %get-tuple-element.417), channel_id=1, source_target_pairs={{0,4},{2,6},{4,0},{6,2},{8,12},{10,14},{12,8},{14,10},{16,20},{18,... | collective-permute-start | bytes 2654216 | tf_op jit(solution)/shard_map/ppermute | solution.py:394
  190.5 22.6 %collective-permute-start.25 = (f32[2,2,48,768]{3,2,1,0:T(8,128)S(1)}, f32[2,2,48,768]{3,2,1,0:T(8,128)}, u32[]{:S(2)}, u32[]{:S(2)}) collective-permute-start(f32[2,2,48,768]{3,2,1,0:T(8,128)S(1)} %get-tuple-element.423), channel_id=1, source_target_pairs={{0,8},{2,10},{4,12},{6,14},{8,0},{10,2},{12,4},{14,6},{16,24},{18,... | collective-permute-start | bytes 1769480 | tf_op jit(solution)/shard_map/ppermute | solution.py:394
  190.5 22.6 %collective-permute-start.27 = (f32[256,768]{1,0:T(8,128)S(1)}, f32[256,768]{1,0:T(8,128)S(1)}, u32[]{:S(2)}, u32[]{:S(2)}) collective-permute-start(f32[256,768]{1,0:T(8,128)S(1)} %copy-done.4), channel_id=1, source_target_pairs={{0,1},{1,0},{2,3},{3,2},{4,5},{5,4},{6,7},{7,6},{8,9},{9,8},{10,11... | collective-permute-start | bytes 2359304 | tf_op jit(solution)/shard_map/ppermute | solution.py:391
  214.0 21.4 %collective-permute-start.30 = (f32[2,2,2,56,768]{4,3,2,1,0:T(8,128)}, f32[2,2,2,56,768]{4,3,2,1,0:T(8,128)}, u32[]{:S(2)}, u32[]{:S(2)}) collective-permute-start(f32[2,2,2,56,768]{4,3,2,1,0:T(8,128)} %get-tuple-element.348), channel_id=1, source_target_pairs={{0,2},{2,0},{4,6},{6,4},{8,10},{10,8},{12,14},{14,12},{16,18},{18,... | collective-permute-start | bytes 4128776 | tf_op jit(solution)/shard_map/ppermute | solution.py:394
  214.1 21.4 %collective-permute-start.32 = (f32[256,768]{1,0:T(8,128)S(1)}, f32[256,768]{1,0:T(8,128)}, u32[]{:S(2)}, u32[]{:S(2)}) collective-permute-start(f32[256,768]{1,0:T(8,128)S(1)} %copy-done.6), channel_id=1, source_target_pairs={{0,1},{1,0},{2,3},{3,2},{4,5},{5,4},{6,7},{7,6},{8,9},{9,8},{10,11... | collective-permute-start | bytes 2359304 | tf_op jit(solution)/shard_map/ppermute | solution.py:391
  215.0 20.5 %collective-permute-start.31 = (f32[2,2,2,56,384]{4,3,2,1,0:T(8,128)}, f32[2,2,2,56,384]{4,3,2,1,0:T(8,128)}, u32[]{:S(2)}, u32[]{:S(2)}) collective-permute-start(f32[2,2,2,56,384]{4,3,2,1,0:T(8,128)} %get-tuple-element.350), channel_id=1, source_target_pairs={{0,2},{2,0},{4,6},{6,4},{8,10},{10,8},{12,14},{14,12},{16,18},{18,... | collective-permute-start | bytes 2064392 | tf_op jit(solution)/shard_map/ppermute | solution.py:394
  216.4 19.1 %collective-permute-start.29 = (f32[2,48,1152]{2,1,0:T(8,128)}, f32[2,48,1152]{2,1,0:T(8,128)}, u32[]{:S(2)}, u32[]{:S(2)}) collective-permute-start(f32[2,48,1152]{2,1,0:T(8,128)} %get-tuple-element.426), channel_id=1, source_target_pairs={{0,8},{2,10},{4,12},{6,14},{8,0},{10,2},{12,4},{14,6},{16,24},{18,... | collective-permute-start | bytes 1327112 | tf_op jit(solution)/shard_map/ppermute | solution.py:394
  237.1 21.6 %collective-permute-start.35 = (f32[2,2,56,768]{3,2,1,0:T(8,128)S(1)}, f32[2,2,56,768]{3,2,1,0:T(8,128)S(1)}, u32[]{:S(2)}, u32[]{:S(2)}) collective-permute-start(f32[2,2,56,768]{3,2,1,0:T(8,128)S(1)} %get-tuple-element.420), channel_id=1, source_target_pairs={{0,4},{2,6},{4,0},{6,2},{8,12},{10,14},{12,8},{14,10},{16,20},{18,... | collective-permute-start | bytes 2064392 | tf_op jit(solution)/shard_map/ppermute | solution.py:394
  237.9 20.9 %collective-permute-start.37 = (f32[256,768]{1,0:T(8,128)S(1)}, f32[256,768]{1,0:T(8,128)S(1)}, u32[]{:S(2)}, u32[]{:S(2)}) collective-permute-start(f32[256,768]{1,0:T(8,128)S(1)} %copy-done), channel_id=1, source_target_pairs={{0,1},{1,0},{2,3},{3,2},{4,5},{5,4},{6,7},{7,6},{8,9},{9,8},{10,11... | collective-permute-start | bytes 2359304 | tf_op jit(solution)/shard_map/ppermute | solution.py:391
  239.6 19.1 %collective-permute-start.36 = (f32[2,2,56,384]{3,2,1,0:T(8,128)S(1)}, f32[2,2,56,384]{3,2,1,0:T(8,128)S(1)}, u32[]{:S(2)}, u32[]{:S(2)}) collective-permute-start(f32[2,2,56,384]{3,2,1,0:T(8,128)S(1)} %get-tuple-element.434), channel_id=1, source_target_pairs={{0,8},{2,10},{4,12},{6,14},{8,0},{10,2},{12,4},{14,6},{16,24},{18,... | collective-permute-start | bytes 1032200 | tf_op jit(solution)/shard_map/ppermute | solution.py:394
  (86 other events, 754.9 us)
Sparse Core Ops, SparseCore 0:
  35.1 66.1 all-gather.1
  137.8 79.9 reduce-scatter.1
